TPU v7x, 512 devices: a whole 4x4x16 slice. The times are simulated.
512 devices in a mesh: seq: 16 (over y, x), mem: 32 (over z, core).
Axes of the slice: x: 4, y: 4, z: 16, core: 2. Of those that a mesh axis runs over, the one named last changes fastest.
Arguments:
- query: bfloat16 [65536, 2048], P(('seq', 'mem')), may hold values from -64 to 64
- key: bfloat16 [65536, 2048], P(('seq', 'mem')), may hold values from -64 to 64
- value: bfloat16 [65536, 2048], P(('seq', 'mem')), may hold values from -6 to 6
- mem_key: bfloat16 [4096, 2048], P('mem'), may hold values from -6 to 6
- mem_value: bfloat16 [4096, 2048], P('mem'), may hold values from -6 to 6
- block_ids: int32 [8192, 2], P(('seq', 'mem')), may hold values from 0 to 31, all different within a row; in each aligned block of 16 rows (0 to 15, 16 to 31, ...) at most 2 rows name the same one
- gate_logit: float32 [16], replicated, may hold values from -2 to 2
- d_out: bfloat16 [65536, 2048], P(('seq', 'mem')), may hold values from -16 to 16
Outputs:
- out: bfloat16 [65536, 2048], P(('seq', 'mem'))
- d_query: bfloat16 [65536, 2048], P(('seq', 'mem'))
- gate_grad: float32 [16], replicated
Inputs may be any that keep to these rules, and one draw needn't show every extreme that they name: `block_ids`: each row names 2 different memory blocks. Among the query groups of one device no block is named by more than 2 rows, and some device names some block exactly 2 times.
All inputs are finite; a program needn't handle non-finite values.
Results may differ from a plain program's by a relative error of at most 0.015.
Values may be sent and summed in bfloat16 or wider, within the bound.
A program may use at most 64 MiB of HBM per device.

v0:
```python
import math

import jax
import jax.numpy as jnp
from jax import lax
from jax.sharding import PartitionSpec as P


def head_split(array, heads):
    return array.reshape(array.shape[0], heads, array.shape[1] // heads)


def body(query, key, value, mem_key, mem_value, block_ids, gate_logit, d_out):
    tok_rows, width = query.shape
    heads = gate_logit.shape[0]
    head_dim = width // heads
    softmax_scale = head_dim ** (-0.5)
    mem_devices = lax.axis_size("mem")
    groups, fetched = block_ids.shape
    group_rows = tok_rows // groups
    capacity = max(2, 2 * tok_rows * fetched // (group_rows * mem_devices))
    slot_count = mem_devices * capacity
    all_tokens = tok_rows * lax.axis_size("seq") * lax.axis_size("mem")
    gate_open = jax.nn.sigmoid(gate_logit)[None, :, None]
    q_heads = head_split(query, heads)
    k_heads = head_split(key, heads)
    v_heads = head_split(value, heads)
    grad_f = head_split(d_out, heads).astype(jnp.float32)
    local_scores = (
        jnp.einsum("qhd,khd->hqk", q_heads, k_heads, preferred_element_type=jnp.float32)
        * softmax_scale
    )
    row_index = lax.broadcasted_iota(jnp.int32, (tok_rows, tok_rows), 0)
    col_index = lax.broadcasted_iota(jnp.int32, (tok_rows, tok_rows), 1)
    local_scores = jnp.where((row_index >= col_index)[None], local_scores, -1e30)
    local_peak = jnp.max(local_scores, axis=-1, keepdims=True)
    local_exp = jnp.exp(local_scores - local_peak)
    local_prob = local_exp / jnp.sum(local_exp, axis=-1, keepdims=True)
    local_out = jnp.einsum(
        "hqk,khd->qhd", local_prob.astype(jnp.bfloat16), v_heads, preferred_element_type=jnp.float32
    )
    pair_owner = block_ids.reshape(groups * fetched)
    owner_hot = (pair_owner[:, None] == jnp.arange(mem_devices, dtype=jnp.int32)[None, :]).astype(
        jnp.int32
    )
    earlier = jnp.cumsum(owner_hot, axis=0) - owner_hot
    pair_slot = pair_owner * capacity + jnp.sum(earlier * owner_hot, axis=1)
    dispatch = (pair_slot[:, None] == jnp.arange(slot_count, dtype=jnp.int32)[None, :]).astype(
        jnp.float32
    )
    to_slots = jnp.transpose(jnp.sum(dispatch.reshape(groups, fetched, slot_count), axis=1))
    to_slots_half = to_slots.astype(jnp.bfloat16)
    dispatch_half = dispatch.astype(jnp.bfloat16)

    def place_rows(rows_half):
        placed = jnp.dot(to_slots_half, rows_half, preferred_element_type=jnp.float32)
        return placed.astype(jnp.bfloat16).reshape(mem_devices, capacity, rows_half.shape[1])

    mem_dout = (gate_open * grad_f).astype(jnp.bfloat16)
    dout_groups = mem_dout.reshape(groups, group_rows * width)
    query_groups = query.reshape(groups, group_rows * width)
    got_query = lax.all_to_all(
        place_rows(query_groups), "mem", split_axis=0, concat_axis=0, tiled=True
    )
    slot_query = got_query.reshape(slot_count, group_rows, heads, head_dim)
    mem_k_heads = head_split(mem_key, heads)
    mem_v_heads = head_split(mem_value, heads)
    mem_scores = (
        jnp.einsum("sqhd,khd->shqk", slot_query, mem_k_heads, preferred_element_type=jnp.float32)
        * softmax_scale
    )
    slot_peak = jnp.max(mem_scores, axis=-1, keepdims=True)
    slot_lse = slot_peak + jnp.log(jnp.sum(jnp.exp(mem_scores - slot_peak), axis=-1, keepdims=True))
    slot_weight = jnp.exp(mem_scores - slot_lse).astype(jnp.bfloat16)
    slot_out = jnp.einsum(
        "shqk,khd->sqhd", slot_weight, mem_v_heads, preferred_element_type=jnp.float32
    ).astype(jnp.bfloat16)
    slot_out_wire = slot_out.reshape(mem_devices, capacity, group_rows * width)
    slot_lse_wire = jnp.transpose(slot_lse[..., 0], (0, 2, 1)).reshape(
        mem_devices, capacity, group_rows * heads
    )
    back_out = lax.all_to_all(slot_out_wire, "mem", split_axis=0, concat_axis=0, tiled=True)
    back_lse = lax.all_to_all(slot_lse_wire, "mem", split_axis=0, concat_axis=0, tiled=True)
    pair_out = jnp.dot(
        dispatch_half,
        back_out.reshape(slot_count, group_rows * width),
        preferred_element_type=jnp.float32,
    )
    pair_lse = jnp.dot(
        dispatch, back_lse.reshape(slot_count, group_rows * heads), precision=lax.Precision.HIGHEST
    )
    pair_lse = pair_lse.reshape(groups, fetched, group_rows, heads)
    lse_peak = jnp.max(pair_lse, axis=1, keepdims=True)
    total_lse = lse_peak + jnp.log(jnp.sum(jnp.exp(pair_lse - lse_peak), axis=1, keepdims=True))
    pair_share = jnp.exp(pair_lse - total_lse)
    pair_view = pair_out.reshape(groups, fetched, group_rows, heads, head_dim)
    mem_out = jnp.sum(pair_share[..., None] * pair_view, axis=1).reshape(tok_rows, heads, head_dim)
    mixed = gate_open * mem_out + (1.0 - gate_open) * local_out
    out = mixed.astype(jnp.bfloat16).reshape(tok_rows, width)
    gate_term = (
        jnp.sum(grad_f * (mem_out - local_out), axis=(0, 2))
        * (gate_open * (1.0 - gate_open))[0, :, 0]
    )
    gate_grad = lax.psum(gate_term, ("seq", "mem")) / math.sqrt(all_tokens)
    local_dout = ((1.0 - gate_open) * grad_f).astype(jnp.bfloat16)
    local_delta = jnp.sum(local_dout.astype(jnp.float32) * local_out, axis=-1)
    local_dp = jnp.einsum("qhd,khd->hqk", local_dout, v_heads, preferred_element_type=jnp.float32)
    local_ds = (local_prob * (local_dp - jnp.transpose(local_delta)[:, :, None])).astype(
        jnp.bfloat16
    )
    local_dq = (
        jnp.einsum("hqk,khd->qhd", local_ds, k_heads, preferred_element_type=jnp.float32)
        * softmax_scale
    )
    mem_delta = jnp.sum(mem_dout.astype(jnp.float32) * mem_out, axis=-1)
    group_stats = jnp.stack([total_lse[:, 0], mem_delta.reshape(groups, group_rows, heads)], axis=1)
    group_stats = group_stats.reshape(groups, 2 * group_rows * heads)
    slot_stats = jnp.dot(to_slots, group_stats, precision=lax.Precision.HIGHEST).reshape(
        mem_devices, capacity, 2 * group_rows * heads
    )
    got_stats = lax.all_to_all(slot_stats, "mem", split_axis=0, concat_axis=0, tiled=True)
    got_grad = lax.all_to_all(
        place_rows(dout_groups), "mem", split_axis=0, concat_axis=0, tiled=True
    )
    slot_grad = got_grad.reshape(slot_count, group_rows, heads, head_dim)
    stats_view = got_stats.reshape(slot_count, 2, group_rows, heads)
    slot_total = jnp.transpose(stats_view[:, 0], (0, 2, 1))[..., None]
    slot_delta = jnp.transpose(stats_view[:, 1], (0, 2, 1))[..., None]
    slot_prob = jnp.exp(mem_scores - slot_total)
    slot_dp = jnp.einsum(
        "sqhd,khd->shqk", slot_grad, mem_v_heads, preferred_element_type=jnp.float32
    )
    slot_ds = (slot_prob * (slot_dp - slot_delta)).astype(jnp.bfloat16)
    slot_dq = (
        jnp.einsum("shqk,khd->sqhd", slot_ds, mem_k_heads, preferred_element_type=jnp.float32)
        * softmax_scale
    )
    slot_dq = slot_dq.astype(jnp.bfloat16).reshape(mem_devices, capacity, group_rows * width)
    back_dq = lax.all_to_all(slot_dq, "mem", split_axis=0, concat_axis=0, tiled=True)
    pair_dq = jnp.dot(
        dispatch_half,
        back_dq.reshape(slot_count, group_rows * width),
        preferred_element_type=jnp.float32,
    )
    mem_dq = jnp.sum(pair_dq.reshape(groups, fetched, group_rows * width), axis=1).reshape(
        tok_rows, width
    )
    d_query = (local_dq.reshape(tok_rows, width) + mem_dq).astype(jnp.bfloat16)
    return (out, d_query, gate_grad)


def solution(mesh):
    placed = (
        P(("seq", "mem"), None),
        P(("seq", "mem"), None),
        P(("seq", "mem"), None),
        P("mem", None),
        P("mem", None),
        P(("seq", "mem"), None),
        P(),
        P(("seq", "mem"), None),
    )
    return jax.shard_map(
        body,
        mesh=mesh,
        in_specs=placed,
        out_specs=(P(("seq", "mem"), None), P(("seq", "mem"), None), P()),
        check_vma=False,
    )
```

profile of v0, /device:TPU:1, one launch (start us, length us, event | category | flops | bytes accessed | tf_op | source)
XLA Modules:
  0.0 577.5 jit_solution(582687897618560494)
XLA Ops:
  4.8 2.7 reshape.218
  7.5 16.9 %all-to-all-start = ((bf16[32,2,16384]{2,1,0:T(2,128)(2,1)}), bf16[32,2,16384]{2,1,0:T(2,128)(2,1)}, u32[]{:S(2)}, u32[]{:S(2)}) async-start(bf16[32,2,16384]{2,1,0:T(2,128)(2,1)} %reshape.218), calls=%async_computation | async-start | bytes 4194304 | tf_op jit(solution)/shard_map/all_to_all | solution.py:62
  25.5 97.5 %all-to-all-done = bf16[32,2,16384]{2,1,0:T(2,128)(2,1)} async-done(((bf16[32,2,16384]{2,1,0:T(2,128)(2,1)}), bf16[32,2,16384]{2,1,0:T(2,128)(2,1)}, u32[]{:S(2)}, u32[]{:S(2)}) %all-to-all-start) | async-done | bytes 2097184 | tf_op jit(solution)/shard_map/all_to_all | solution.py:62
  123.1 3.3 reshape.219
  128.0 2.4 fusion.4
  131.5 5.2 all-to-all-start.1
  136.7 3.1 convert_bitcast_fusion
  139.9 2.4 copy.232
  144.4 4.5 all-to-all-done.1
  148.8 7.9 %all-to-all-start.2 = ((bf16[32,2,16384]{2,1,0:T(2,128)(2,1)}), bf16[32,2,16384]{2,1,0:T(2,128)(2,1)S(1)}, u32[]{:S(2)}, u32[]{:S(2)}) async-start(bf16[32,2,16384]{2,1,0:T(2,128)(2,1)} %reshape.224), calls=%async_computation.2 | async-start | bytes 4194304 | tf_op jit(solution)/shard_map/all_to_all | solution.py:82
  157.9 2.4 mul.129
  161.5 3.7 convolution_convert_fusion
  165.1 4.4 reshape.234
  169.5 85.8 %all-to-all-done.2 = bf16[32,2,16384]{2,1,0:T(2,128)(2,1)S(1)} async-done(((bf16[32,2,16384]{2,1,0:T(2,128)(2,1)}), bf16[32,2,16384]{2,1,0:T(2,128)(2,1)S(1)}, u32[]{:S(2)}, u32[]{:S(2)}) %all-to-all-start.2) | async-done | bytes 2097184 | tf_op jit(solution)/shard_map/all_to_all | solution.py:82
  256.6 5.2 all-to-all-start.4
  263.9 4.2 reshape.225
  268.0 2.2 copy.290
  275.0 85.4 %all-to-all-done.4 = bf16[32,2,16384]{2,1,0:T(2,128)(2,1)S(1)} async-done(((bf16[32,2,16384]{2,1,0:T(2,128)(2,1)}), bf16[32,2,16384]{2,1,0:T(2,128)(2,1)S(1)}, u32[]{:S(2)}, u32[]{:S(2)}) %all-to-all-start.4) | async-done | bytes 2097184 | tf_op jit(solution)/shard_map/all_to_all | solution.py:122
  360.4 5.1 all-to-all-start.3
  365.6 2.8 reshape.235
  368.4 10.2 %all-to-all-done.3 = f32[32,2,256]{2,1,0:T(2,128)S(1)} async-done(((f32[32,2,256]{2,1,0:T(2,128)}), f32[32,2,256]{2,1,0:T(2,128)S(1)}, u32[]{:S(2)}, u32[]{:S(2)}) %all-to-all-start.3) | async-done | bytes 65568 | tf_op jit(solution)/shard_map/all_to_all | solution.py:121
  379.9 6.0 %fusion.26 = bf16[64,8,16,128]{3,1,0,2:T(8,128)(2,1)} fusion(f32[16,64,8,128]{3,2,1,0:T(8,128)} %copy-done.1, bf16[64,8,16,128]{3,2,1,0:T(8,128)(2,1)} %reshape.235, f32[64,16,8]{2,0,1:T(8,128)S(1)} %copy.257, f32[64,16,8]{2,0,1:T(8,128)S(1)} %copy.253, bf16[128,16,128,1]{2,1,0,3:T(8,128)(2,1)} %bitcast.192, bf16[128,16,128,1]{2,1,0,3:T(8,128)(2,1)S(1)} %bitcast.182), kind=kOutput, calls=%fused_computation.30 | convolution fusion | flops 544210944 | bytes 9502720 | tf_op jit(solution)/shard_map/shqk,khd->sqhd/dot_general | solution.py:135
  385.9 4.0 copy.259
  392.0 5.3 all-to-all-start.5
  404.2 2.6 copy.235
  406.8 4.1 multiply_reduce_fusion.1
  410.9 151.6 %psum.7 = f32[16]{0:T(128)S(1)} all-reduce(f32[16]{0:T(128)S(1)} %multiply_multiply_fusion), channel_id=1, replica_groups=mesh['seq'=16,'mem'=32] {'seq','mem'}, use_global_device_ids=true, to_apply=%region_14.15 | all-reduce | flops 16 | bytes 128 | tf_op jit(solution)/shard_map/psum | solution.py:104
  562.5 3.0 convolution_multiply_fusion
  565.5 2.6 copy.260
  569.7 2.2 reshape.251
  571.9 2.3 convolution_reduce_fusion
  575.4 2.1 add_convert_fusion
  (86 shorter events, 33.3 us)
Async XLA Ops:
  0.6 406.1 %copy-start = (bf16[128,2048]{1,0:T(8,128)(2,1)S(1)}, bf16[128,2048]{1,0:T(8,128)(2,1)}, u32[]{:S(2)}) copy-start(bf16[128,2048]{1,0:T(8,128)(2,1)} %param.10) | copy-start | bytes 1572868
  7.5 17.0 %copy-start.11 = (bf16[128,2048]{1,0:T(8,128)(2,1)S(1)}, bf16[128,2048]{1,0:T(8,128)(2,1)}, u32[]{:S(2)}) copy-start(bf16[128,2048]{1,0:T(8,128)(2,1)} %param.11) | copy-start | bytes 1572868
  7.5 17.1 %copy-start.12 = (bf16[128,2048]{1,0:T(8,128)(2,1)S(1)}, bf16[128,2048]{1,0:T(8,128)(2,1)}, u32[]{:S(2)}) copy-start(bf16[128,2048]{1,0:T(8,128)(2,1)} %param.12) | copy-start | bytes 1572868
  7.5 115.6 %all-to-all-start = ((bf16[32,2,16384]{2,1,0:T(2,128)(2,1)}), bf16[32,2,16384]{2,1,0:T(2,128)(2,1)}, u32[]{:S(2)}, u32[]{:S(2)}) async-start(bf16[32,2,16384]{2,1,0:T(2,128)(2,1)} %reshape.218), calls=%async_computation | async-start | bytes 4194304 | tf_op jit(solution)/shard_map/all_to_all | solution.py:62
  24.6 101.8 %copy-start.9 = (bf16[16,8,16,128]{3,2,1,0:T(8,128)(2,1)}, bf16[16,8,16,128]{3,2,1,0:T(8,128)(2,1)S(1)}, u32[]{:S(2)}) copy-start(bf16[16,8,16,128]{3,2,1,0:T(8,128)(2,1)S(1)} %copy.288) | copy-start | bytes 1572868
  128.0 2.4 copy-start.1
  130.4 6.4 %copy-start.13 = (bf16[16,8,16,128]{3,2,1,0:T(8,128)(2,1)S(1)}, bf16[16,8,16,128]{3,2,1,0:T(8,128)(2,1)}, u32[]{:S(2)}) copy-start(bf16[16,8,16,128]{3,2,1,0:T(8,128)(2,1)} %copy.289) | copy-start | bytes 1572868
  131.5 17.3 %all-to-all-start.1 = ((f32[32,2,128]{2,1,0:T(2,128)}), f32[32,2,128]{2,1,0:T(2,128)S(1)}, u32[]{:S(2)}, u32[]{:S(2)}) async-start(f32[32,2,128]{2,1,0:T(2,128)} %reshape.221), calls=%async_computation.1 | async-start | bytes 65536 | tf_op jit(solution)/shard_map/all_to_all | solution.py:83
  144.4 12.3 %copy-start.15 = (f32[16]{0:T(128)S(1)}, f32[16]{0:T(128)}, u32[]{:S(2)}) copy-start(f32[16]{0:T(128)} %param.14) | copy-start | bytes 196
  148.8 106.5 %all-to-all-start.2 = ((bf16[32,2,16384]{2,1,0:T(2,128)(2,1)}), bf16[32,2,16384]{2,1,0:T(2,128)(2,1)S(1)}, u32[]{:S(2)}, u32[]{:S(2)}) async-start(bf16[32,2,16384]{2,1,0:T(2,128)(2,1)} %reshape.224), calls=%async_computation.2 | async-start | bytes 4194304 | tf_op jit(solution)/shard_map/all_to_all | solution.py:82
  156.7 3.6 copy-start.3
  255.3 1.3 copy-start.2
  256.6 103.8 %all-to-all-start.4 = ((bf16[32,2,16384]{2,1,0:T(2,128)(2,1)}), bf16[32,2,16384]{2,1,0:T(2,128)(2,1)S(1)}, u32[]{:S(2)}, u32[]{:S(2)}) async-start(bf16[32,2,16384]{2,1,0:T(2,128)(2,1)} %reshape.234), calls=%async_computation.4 | async-start | bytes 4194304 | tf_op jit(solution)/shard_map/all_to_all | solution.py:122
  270.2 3.0 copy-start.6
  272.1 1.1 copy-start.4
  360.4 18.2 %all-to-all-start.3 = ((f32[32,2,256]{2,1,0:T(2,128)}), f32[32,2,256]{2,1,0:T(2,128)S(1)}, u32[]{:S(2)}, u32[]{:S(2)}) async-start(f32[32,2,256]{2,1,0:T(2,128)} %copy.252), calls=%async_computation.3 | async-start | bytes 131072 | tf_op jit(solution)/shard_map/all_to_all | solution.py:121
  368.4 11.5 %copy-start.10 = (bf16[16,8,16,128]{3,2,1,0:T(8,128)(2,1)S(1)}, bf16[16,8,16,128]{3,2,1,0:T(8,128)(2,1)}, u32[]{:S(2)}) copy-start(bf16[16,8,16,128]{3,2,1,0:T(8,128)(2,1)} %copy-done.9) | copy-start | bytes 1572868
  392.0 177.6 %all-to-all-start.5 = ((bf16[32,2,16384]{2,1,0:T(2,128)(2,1)}), bf16[32,2,16384]{2,1,0:T(2,128)(2,1)S(1)}, u32[]{:S(2)}, u32[]{:S(2)}) async-start(bf16[32,2,16384]{2,1,0:T(2,128)(2,1)} %reshape.236), calls=%async_computation.5 | async-start | bytes 4194304 | tf_op jit(solution)/shard_map/all_to_all | solution.py:139
  399.8 3.0 copy-start.5
  401.5 2.7 copy-start.8
  565.5 2.6 copy-start.14
  571.9 3.5 copy-start.7
where the time goes:
time: 579 us; the launch traced here: 578 us
  waiting for transfers between devices  283 us (49%)
  blocking collectives  152 us (26%)
  local copies, waits for them, and re-layouts  58.8 us (10%)
  starting transfers between devices  45.5 us (8%)
  matrix products  28.6 us (5%)
  other arithmetic  8.47 us (1%)
    psum x1, blocking collectives, body(): gate_grad = lax.psum(gate_term, ('seq', 'mem')) / math.sqrt(all_tokens)  152 us
    all_to_all x1, waiting for transfers between devices, body(): lax.all_to_all(place_rows(query_groups), 'mem', split_axis=0, concat_axis...  97.5 us
    all_to_all x1, waiting for transfers between devices, body(): lax.all_to_all(slot_out_wire, 'mem', split_axis=0, concat_axis=0, tiled=T...  85.8 us
    all_to_all x1, waiting for transfers between devices, body(): lax.all_to_all(place_rows(dout_groups), 'mem', split_axis=0, concat_axis=...  85.4 us
    all_to_all x1, starting transfers between devices, body(): lax.all_to_all(place_rows(query_groups), 'mem', split_axis=0, concat_axis...  16.9 us
  transfers between devices with their start and end apart: 6, of which 5 were waited for; matrix products, arithmetic and copies ran while one was open for 10% of the time, Pallas kernels for 0%

commit v1 on v0

v1 whole, which is shorter than its diff:
```python
import functools
import math

import jax
import jax.numpy as jnp
from jax import lax
from jax.experimental import pallas as pl
from jax.experimental.pallas import tpu as pltpu
from jax.sharding import PartitionSpec as P

NX = 4
MESH = pl.DeviceIdType.MESH
HD = 128
F32 = jnp.float32
BF16 = jnp.bfloat16


def dot_nt(a, b):
    return lax.dot_general(a, b, (((1,), (1,)), ((), ())), preferred_element_type=F32)


def dot_nn(a, b):
    return jnp.dot(a, b, preferred_element_type=F32)


def kernel(
    nz, total_tokens,
    q_hbm, k_hbm, v_hbm, mk_hbm, mv_hbm, d_hbm, ids_ref, gl_ref,
    out_hbm, dq_hbm, gg_ref,
    kb, vb, qs, ks, vs, gs, md, qg, mg, po, da, db, ls, dl, lo, ldq, so, sd, gx, codes, codes_sm,
    rc, rx, ry, rz,
    loc, swap_s, swap_r, res_s, res_r,
    zk_s, zk_r, zv_s, zv_r,
    xa_s, xa_r, xb_s, xb_r, xc_s, xc_r, xd_s, xd_r,
    ya_s, ya_r, yb_s, yb_r, yc_s, yc_r, yd_s, yd_r,
    rc_s, rc_r, rx_s, rx_r, ry_s, ry_r, rz_s, rz_r,
):
    rows = q_hbm.shape[0]
    half = q_hbm.shape[1] // 2
    heads = half // HD
    groups = ids_ref.shape[0]
    gr = rows // groups
    quarter = 2 * rows // NX
    eighth = quarter // 2
    scale = HD ** -0.5

    s = lax.axis_index("seq")
    m = lax.axis_index("mem")
    x, y = lax.rem(s, NX), s // NX
    z, c = m // 2, lax.rem(m, 2)
    other = 1 - c

    def at_x(step):
        return (y * NX + lax.rem(x + step + NX, NX), m)

    def at_y(step):
        return (lax.rem(y + step + NX, NX) * NX + x, m)

    def at_z(step):
        return (s, lax.rem(z + step + nz, nz) * 2 + c)

    sib = (s, z * 2 + other)

    mine = pl.ds(pl.multiple_of(c * half, half), half)
    theirs = pl.ds(pl.multiple_of(other * half, half), half)
    my_rows = pl.ds(pl.multiple_of(c * rows, rows), rows)
    sib_rows = pl.ds(pl.multiple_of(other * rows, rows), rows)

    pairs = [(mk_hbm, kb.at[z]), (mv_hbm, vb.at[z]), (q_hbm, qs), (d_hbm, gs), (k_hbm, ks), (v_hbm, vs)]
    own = [
        pltpu.make_async_copy(src.at[:, mine], dst.at[my_rows], loc.at[i])
        for i, (src, dst) in enumerate(pairs)
    ]
    for cp in own:
        cp.start()

    barrier = pltpu.get_barrier_semaphore()

    def greet(dev):
        pl.semaphore_signal(barrier, inc=1, device_id=dev, device_id_type=MESH)

    greet(sib)
    for step in range(1, NX):
        greet(at_x(step))
        greet(at_y(step))

    def greet_z(step, carry):
        greet(at_z(step))
        return carry

    lax.fori_loop(1, nz, greet_z, 0)

    a0 = jnp.broadcast_to(ids_ref[:, 0:1], (groups, rows))
    a1 = jnp.broadcast_to(ids_ref[:, 1:2], (groups, rows))
    g_row = lax.broadcasted_iota(jnp.int32, (groups, rows), 0)
    g_tok = lax.broadcasted_iota(jnp.int32, (groups, rows), 1) // gr
    zero = jnp.zeros((groups, rows), jnp.int32)
    here = g_row == g_tok
    i0 = jnp.sum(jnp.where(here, a0, zero), axis=0, keepdims=True)
    i1 = jnp.sum(jnp.where(here, a1, zero), axis=0, keepdims=True)
    one = zero + 1
    earlier = g_row < g_tok
    r0 = jnp.sum(jnp.where(earlier & ((a0 == i0) | (a1 == i0)), one, zero), axis=0, keepdims=True)
    r1 = jnp.sum(jnp.where(earlier & ((a0 == i1) | (a1 == i1)), one, zero), axis=0, keepdims=True)
    code0 = i0 * 4 + c * 2 + r0
    code1 = i1 * 4 + c * 2 + r1
    first = lax.broadcasted_iota(jnp.int32, (8, rows), 0) == 0
    codes[c] = jnp.where(first, jnp.broadcast_to(code0, (8, rows)), jnp.broadcast_to(code1, (8, rows)))

    for j in range(heads):
        logit = jnp.full((8, HD), gl_ref[c * heads + j], F32)
        gx[:, j * HD:(j + 1) * HD] = 1.0 / (1.0 + jnp.exp(-logit))

    pl.semaphore_wait(barrier, 1 + 2 * (NX - 1) + nz - 1)

    swaps = [
        pltpu.make_async_remote_copy(
            src_ref=src.at[:, theirs], dst_ref=dst.at[my_rows],
            send_sem=swap_s.at[i], recv_sem=swap_r.at[i], device_id=sib, device_id_type=MESH,
        )
        for i, (src, dst) in enumerate(pairs)
    ]
    code_swap = pltpu.make_async_remote_copy(
        src_ref=codes.at[c], dst_ref=codes.at[c],
        send_sem=swap_s.at[6], recv_sem=swap_r.at[6], device_id=sib, device_id_type=MESH,
    )
    swaps[0].start()
    swaps[1].start()
    code_swap.start()
    for cp in swaps[2:]:
        cp.start()

    def got_swap(i):
        own[i].wait()
        pltpu.make_async_remote_copy(
            src_ref=pairs[i][0].at[:, mine], dst_ref=pairs[i][1].at[sib_rows],
            send_sem=swap_s.at[i], recv_sem=swap_r.at[i], device_id=sib, device_id_type=MESH,
        ).wait_recv()

    def part(buf, o, row, count):
        return buf.at[o, pl.ds(pl.multiple_of(row, count), count)]

    def push(buf, o, row, count, send, recv, dev):
        return pltpu.make_async_remote_copy(
            src_ref=part(buf, o, row, count), dst_ref=part(buf, o, row, count),
            send_sem=send, recv_sem=recv, device_id=dev, device_id_type=MESH,
        )

    def k_z(o, j, step):
        return push(kb, o, x * quarter, quarter, zk_s.at[j], zk_r.at[j], at_z(step))

    def v_z(o, j, step):
        return push(vb, o, y * quarter, quarter, zv_s.at[j], zv_r.at[j], at_z(step))

    def origin(n):
        away = (n + 1) // 2
        return lax.rem(z + nz + jnp.where(lax.rem(n, 2) == 1, -away, away), nz)

    last = nz - 1

    def forward_z(n, o):
        odd = lax.rem(n, 2) == 1

        @pl.when(odd & (n + 2 <= last))
        def _():
            k_z(o, n + 2, 1).start()

        @pl.when(odd & (n + 2 < last))
        def _():
            v_z(o, n + 2, 1).start()

        @pl.when(jnp.logical_not(odd) & (n + 2 < last))
        def _():
            k_z(o, n + 2, -1).start()

        @pl.when(jnp.logical_not(odd) & (n + 1 <= last))
        def _():
            v_z(o, jnp.minimum(n + 2, last), -1).start()

    def ring(buf, n, o, place, at, sa, ra, sb, rb, sc, rc_, sd_, rd):
        left = lax.rem(place + NX - 1, NX)
        right = lax.rem(place + 1, NX)
        far = lax.rem(place + 2, NX)
        to_right = lambda: push(buf, o, place * quarter, quarter, sa.at[n], ra.at[n], at(1))
        to_left = lambda: push(buf, o, place * quarter, quarter, sb.at[n], rb.at[n], at(-1))
        from_left = lambda: push(buf, o, left * quarter, quarter, sa.at[n], ra.at[n], at(1))
        from_right = lambda: push(buf, o, right * quarter, quarter, sb.at[n], rb.at[n], at(-1))
        on_right = lambda: push(buf, o, left * quarter, eighth, sc.at[n], rc_.at[n], at(1))
        on_left = lambda: push(buf, o, right * quarter + eighth, eighth, sd_.at[n], rd.at[n], at(-1))
        far_left = lambda: push(buf, o, far * quarter, eighth, sc.at[n], rc_.at[n], at(1))
        far_right = lambda: push(buf, o, far * quarter + eighth, eighth, sd_.at[n], rd.at[n], at(-1))
        return to_right, to_left, from_left, from_right, on_right, on_left, far_left, far_right

    def x_ring(n, o):
        return ring(kb, n, o, x, at_x, xa_s, xa_r, xb_s, xb_r, xc_s, xc_r, xd_s, xd_r)

    def y_ring(n, o):
        return ring(vb, n, o, y, at_y, ya_s, ya_r, yb_s, yb_r, yc_s, yc_r, yd_s, yd_r)

    def arrive(n):
        o = origin(n)
        k_z(o, n, 1).wait_recv()
        v_z(o, n, 1).wait_recv()
        forward_z(n, o)
        xr, yr = x_ring(n, o), y_ring(n, o)
        xr[0]().start()
        yr[0]().start()
        xr[1]().start()
        yr[1]().start()

    def relay(n):
        o = origin(n)
        xr, yr = x_ring(n, o), y_ring(n, o)
        xr[2]().wait_recv()
        xr[4]().start()
        xr[3]().wait_recv()
        xr[5]().start()
        yr[2]().wait_recv()
        yr[4]().start()
        yr[3]().wait_recv()
        yr[5]().start()

    def settle(n):
        o = origin(n)
        xr, yr = x_ring(n, o), y_ring(n, o)
        xr[6]().wait_recv()
        xr[7]().wait_recv()
        yr[6]().wait_recv()
        yr[7]().wait_recv()

    def drain(n, carry):
        o = origin(n)
        k_z(o, n, 1).wait_send()
        v_z(o, n, 1).wait_send()
        xr, yr = x_ring(n, o), y_ring(n, o)
        for r in (xr, yr):
            r[0]().wait_send()
            r[1]().wait_send()
            r[4]().wait_send()
            r[5]().wait_send()
        return carry

    slot_rows = 4 * gr

    def attend(n):
        o = origin(n)
        for blk in range(2):
            r0_ = pl.ds(pl.multiple_of((o * 2 + blk) * slot_rows, slot_rows), slot_rows)
            sl = pl.ds((o * 2 + blk) * 4, 4)
            cube = (4, gr, HD)
            for h in range(heads):
                cols = slice(h * HD, (h + 1) * HD)
                kk = kb[o, blk * rows:(blk + 1) * rows, cols]
                vv = vb[o, blk * rows:(blk + 1) * rows, cols]
                sc = dot_nt(qg[r0_, cols], kk) * scale
                peak = jnp.max(sc, axis=-1, keepdims=True)
                e = jnp.exp(sc - peak)
                tot = jnp.sum(e, axis=-1, keepdims=True)
                p = e / tot
                dp = dot_nt(mg[r0_, cols], vv)
                delta = jnp.sum(p * dp, axis=-1, keepdims=True)
                pb = p.astype(BF16)
                dsb = (p * (dp - delta)).astype(BF16)
                po[sl, :, cols] = dot_nn(pb, vv).reshape(cube)
                ab = dot_nn(jnp.concatenate([dsb, pb], axis=0), kk)
                da[sl, :, cols] = ab[:slot_rows].reshape(cube)
                db[sl, :, cols] = ab[slot_rows:].reshape(cube)
                ls[sl, :, cols] = jnp.broadcast_to(peak + jnp.log(tot), (slot_rows, HD)).reshape(cube)
                dl[sl, :, cols] = jnp.broadcast_to(delta, (slot_rows, HD)).reshape(cube)

    def pick():
        lane = lax.rem(lax.broadcasted_iota(jnp.int32, (1, 2 * rows), 1), gr)
        c0 = jnp.concatenate([codes[0, 0:1, :], codes[1, 0:1, :]], axis=1) * gr + lane
        c1 = jnp.concatenate([codes[0, 1:2, :], codes[1, 1:2, :]], axis=1) * gr + lane
        chunk = 128

        def step(i, carry):
            r = lax.broadcasted_iota(jnp.int32, (chunk, 2 * rows), 0) + i * chunk
            hot = jnp.where((r == c0) | (r == c1), 1.0, 0.0).astype(BF16)
            at = pl.ds(pl.multiple_of(i * chunk, chunk), chunk)
            qg[at, :] = dot_nn(hot, qs[...]).astype(BF16)
            mg[at, :] = dot_nn(hot, md[...]).astype(BF16)
            return carry

        lax.fori_loop(0, qg.shape[0] // chunk, step, 0)

    def local(i, carry):
        at = pl.ds(pl.multiple_of(i * rows, rows), rows)
        ri = lax.broadcasted_iota(jnp.int32, (rows, rows), 0)
        ci = lax.broadcasted_iota(jnp.int32, (rows, rows), 1)
        for h in range(heads):
            cols = slice(h * HD, (h + 1) * HD)
            kk, vv = ks[at, cols], vs[at, cols]
            sc = jnp.where(ri >= ci, dot_nt(qs[at, cols], kk) * scale, -1e30)
            e = jnp.exp(sc - jnp.max(sc, axis=-1, keepdims=True))
            p = e / jnp.sum(e, axis=-1, keepdims=True)
            o = dot_nn(p.astype(BF16), vv)
            ld = ((1.0 - gx[0:1, cols]) * gs[at, cols].astype(F32)).astype(BF16)
            delta = jnp.sum(ld.astype(F32) * o, axis=-1, keepdims=True)
            ds = (p * (dot_nt(ld, vv) - delta)).astype(BF16)
            lo[at, cols] = o
            ldq[at, cols] = dot_nn(ds, kk) * scale
        return carry

    got_swap(0)
    k_z(z, 1, 1).start()
    k_z(z, 2, -1).start()
    got_swap(1)
    v_z(z, 1, 1).start()
    v_z(z, 2, -1).start()

    got_swap(2)
    got_swap(3)
    pltpu.make_async_remote_copy(
        src_ref=codes.at[other], dst_ref=codes.at[other],
        send_sem=swap_s.at[6], recv_sem=swap_r.at[6], device_id=sib, device_id_type=MESH,
    ).wait_recv()
    to_smem = pltpu.make_async_copy(codes, codes_sm, loc.at[6])
    to_smem.start()
    md[...] = (gx[0:1, :] * gs[...].astype(F32)).astype(BF16)
    pick()
    to_smem.wait()
    got_swap(4)
    got_swap(5)

    relay_lag, settle_lag = 2, 4

    def turn(n, carry):
        @pl.when(n <= last)
        def _():
            arrive(n)

        @pl.when(n == 2)
        def _():
            lax.fori_loop(0, 2, local, 0)

        @pl.when((n > relay_lag) & (n - relay_lag <= last))
        def _():
            relay(n - relay_lag)

        @pl.when(n > settle_lag)
        def _():
            settle(n - settle_lag)

        @pl.when(n >= settle_lag)
        def _():
            attend(n - settle_lag)

        return carry

    lax.fori_loop(1, last + settle_lag + 1, turn, 0)

    def blend(g, base, at, second):
        d0, d1 = codes_sm[base, 0, g * gr], codes_sm[base, 1, g * gr]
        l0, l1 = ls[d0], ls[d1]
        peak = jnp.maximum(l0, l1)
        e0, e1 = jnp.exp(l0 - peak), jnp.exp(l1 - peak)
        inv = 1.0 / (e0 + e1)
        s0, s1 = e0 * inv, e1 * inv
        mo = s0 * po[d0] + s1 * po[d1]
        own_rows = slice(gr, 2 * gr) if second else slice(0, gr)
        prod = md[at, :].astype(F32)[own_rows] * mo
        delta = jnp.concatenate(
            [
                jnp.broadcast_to(
                    jnp.sum(prod[:, h * HD:(h + 1) * HD], axis=-1, keepdims=True), (gr, HD)
                )
                for h in range(heads)
            ],
            axis=1,
        )
        dq = s0 * (da[d0] + (dl[d0] - delta) * db[d0])
        dq = dq + s1 * (da[d1] + (dl[d1] - delta) * db[d1])
        return mo, dq * scale

    def mix(i, acc):
        base = i // (groups // 2)
        base = jnp.where(base == 0, other, c)
        g = lax.rem(i, groups // 2) * 2
        at = pl.ds(pl.multiple_of(base * rows + g * gr, 2 * gr), 2 * gr)
        ma, qa = blend(g, base, at, False)
        mb, qb = blend(g + 1, base, at, True)
        mo = jnp.concatenate([ma, mb], axis=0)
        dq = jnp.concatenate([qa, qb], axis=0)
        gate = gx[0:1, :]
        loc_o = lo[at, :]
        so[at, :] = (gate * mo + (1.0 - gate) * loc_o).astype(BF16)
        sd[at, :] = (ldq[at, :] + dq).astype(BF16)
        t = gs[at, :].astype(F32) * (mo - loc_o)
        return acc + t[:gr] + t[gr:]

    acc = jnp.zeros((gr, half), F32)
    acc = lax.fori_loop(0, groups // 2, mix, acc)
    back = []
    for i, (stage, result) in enumerate(((so, out_hbm), (sd, dq_hbm))):
        cp = pltpu.make_async_remote_copy(
            src_ref=stage.at[sib_rows], dst_ref=result.at[:, mine],
            send_sem=res_s.at[i], recv_sem=res_r.at[i], device_id=sib, device_id_type=MESH,
        )
        cp.start()
        back.append(cp)
    acc = lax.fori_loop(groups // 2, groups, mix, acc)
    keep = []
    for i, (stage, result) in enumerate(((so, out_hbm), (sd, dq_hbm))):
        cp = pltpu.make_async_copy(stage.at[my_rows], result.at[:, mine], loc.at[i])
        cp.start()
        keep.append(cp)

    lane = lax.broadcasted_iota(jnp.int32, (8, HD), 1)
    term = jnp.zeros((8, HD), F32)
    for j in range(heads):
        cols = slice(j * HD, (j + 1) * HD)
        tot = jnp.sum(jnp.sum(acc[:, cols], axis=1, keepdims=True), axis=0, keepdims=True)
        gate = gx[:, cols]
        val = jnp.broadcast_to(tot, (8, HD)) * gate * (1.0 - gate)
        term = jnp.where(lane == c * heads + j, val, term)
    term = term * (1.0 / math.sqrt(total_tokens))

    def exchange(buf, place, steps, at, send, recv):
        size = buf.shape[0]

        def make(step):
            return pltpu.make_async_remote_copy(
                src_ref=buf.at[place], dst_ref=buf.at[place],
                send_sem=send.at[step], recv_sem=recv.at[step],
                device_id=at(step), device_id_type=MESH,
            )

        def start(step, carry):
            make(step).start()
            return carry

        def wait(step, carry):
            src = lax.rem(place + size - step, size)
            pltpu.make_async_remote_copy(
                src_ref=buf.at[src], dst_ref=buf.at[src],
                send_sem=send.at[step], recv_sem=recv.at[step],
                device_id=at(step), device_id_type=MESH,
            ).wait_recv()
            make(step).wait_send()
            return carry

        lax.fori_loop(1, steps + 1, start, 0)
        lax.fori_loop(1, steps + 1, wait, 0)
        out = buf[0]
        for i in range(1, size):
            out = out + buf[i]
        return out

    rc[c] = term
    term = exchange(rc, c, 1, lambda step: sib, rc_s, rc_r)
    rx[x] = term
    term = exchange(rx, x, NX - 1, at_x, rx_s, rx_r)
    ry[y] = term
    term = exchange(ry, y, NX - 1, at_y, ry_s, ry_r)
    rz[z] = term
    term = exchange(rz, z, nz - 1, at_z, rz_s, rz_r)
    gg_ref[...] = term

    for cp in keep:
        cp.wait()
    for i, result in enumerate((out_hbm, dq_hbm)):
        pltpu.make_async_remote_copy(
            src_ref=so.at[my_rows], dst_ref=result.at[:, theirs],
            send_sem=res_s.at[i], recv_sem=res_r.at[i], device_id=sib, device_id_type=MESH,
        ).wait_recv()
        back[i].wait_send()
    for cp in swaps:
        cp.wait_send()
    code_swap.wait_send()
    lax.fori_loop(1, nz, drain, 0)


def body(total_tokens, query, key, value, mem_key, mem_value, block_ids, gate_logit, d_out):
    rows, width = query.shape
    half = width // 2
    nz = lax.axis_size("mem") // 2
    gr = rows // block_ids.shape[0]
    slots = 2 * nz * 4 * gr
    dma = pltpu.SemaphoreType.DMA
    any_ = pl.BlockSpec(memory_space=pl.ANY)
    vmem = pl.BlockSpec(memory_space=pltpu.VMEM)
    smem = pl.BlockSpec(memory_space=pltpu.SMEM)
    heads = width // HD
    scratch = (
        [pltpu.VMEM((nz, 2 * rows, half), BF16)] * 2
        + [pltpu.VMEM((2 * rows, half), BF16)] * 5
        + [pltpu.VMEM((slots, half), BF16)] * 2
        + [pltpu.VMEM((slots // gr, gr, half), F32)] * 5
        + [pltpu.VMEM((2 * rows, half), F32)] * 2
        + [pltpu.VMEM((2 * rows, half), BF16)] * 2
        + [pltpu.VMEM((8, half), F32)]
        + [pltpu.VMEM((2, 8, rows), jnp.int32), pltpu.SMEM((2, 8, rows), jnp.int32)]
        + [pltpu.VMEM((size, 8, HD), F32) for size in (2, NX, NX, nz)]
        + [dma((7,)), dma((7,)), dma((7,)), dma((2,)), dma((2,))]
        + [dma((nz,))] * 20
        + [dma((size,)) for size in (2, 2, NX, NX, NX, NX, nz, nz)]
    )
    out, d_query, gate = pl.pallas_call(
        functools.partial(kernel, nz, total_tokens),
        out_shape=(
            jax.ShapeDtypeStruct((rows, width), BF16),
            jax.ShapeDtypeStruct((rows, width), BF16),
            jax.ShapeDtypeStruct((8, HD), F32),
        ),
        in_specs=[any_] * 6 + [vmem, smem],
        out_specs=(any_, any_, vmem),
        scratch_shapes=scratch,
        compiler_params=pltpu.CompilerParams(
            collective_id=0, has_side_effects=True, vmem_limit_bytes=58 * 1024 * 1024
        ),
    )(query, key, value, mem_key, mem_value, d_out, block_ids, gate_logit)
    return out, d_query, gate[0, :heads]


def solution(mesh):
    tokens = P(("seq", "mem"), None)

    def run(query, *rest):
        return jax.shard_map(
            functools.partial(body, query.shape[0]),
            mesh=mesh,
            in_specs=(tokens, tokens, tokens, P("mem", None), P("mem", None), tokens, P(), tokens),
            out_specs=(tokens, tokens, P()),
            check_vma=False,
        )(query, *rest)

    return run
```

time: 579 us -> 150 us (0.26)
  waiting for transfers between devices: 283 us -> 0 us
  blocking collectives: 152 us -> 0 us
  Pallas kernels: 0 us -> 144 us
  local copies, waits for them, and re-layouts: 58.8 us -> 5.27 us
  starting transfers between devices: 45.5 us -> 0 us
  matrix products: 28.6 us -> 0 us
  other arithmetic: 8.47 us -> 0 us
    all_to_all x6 -> x0, waiting for transfers between devices: 283 us -> none  [the longest x1 97.5 us: body(): lax.all_to_all(place_rows(query_groups), 'mem', split_axis=0, concat_axis...]
    psum x1 -> x0, blocking collectives: 152 us -> none  [body(): gate_grad = lax.psum(gate_term, ('seq', 'mem')) / math.sqrt(all_tokens)]
    pallas_call x0 -> x1, Pallas kernels: none -> 144 us  [body(): pl.pallas_call(functools.partial(kernel, nz, total_tokens), out_shape=(ja...]
    all_to_all x6 -> x0, starting transfers between devices: 45.5 us -> none  [the longest x1 16.9 us: body(): lax.all_to_all(place_rows(query_groups), 'mem', split_axis=0, concat_axis...]
    reshape x16 -> x0, local copies, waits for them, and re-layouts: 33.8 us -> none  [the longest x2 7.07 us: place_rows(): placed.astype(jnp.bfloat16)]
    dot_general x12 -> x0, matrix products: 28.6 us -> none  [the longest x1 6 us: body(): jnp.einsum('shqk,khd->sqhd', slot_ds, mem_k_heads, preferred_element_type...]
    convert_element_type x4 -> x0, local copies, waits for them, and re-layouts: 8.83 us -> none  [the longest x1 4.02 us: body(): slot_dq.astype(jnp.bfloat16)]
  transfers between devices with their start and end apart: 6 -> 0, of which waited for: 5 -> 0; matrix products, arithmetic and copies ran while one was open for 10% -> 0% of each run, Pallas kernels for 0% -> 0%
where the time goes in v1:
time: 150 us
  Pallas kernels  144 us (96%)
  local copies, waits for them, and re-layouts  5.27 us (4%)
    pallas_call x1, Pallas kernels, body(): pl.pallas_call(functools.partial(kernel, nz, total_tokens), out_shape=(ja...  144 us
    unnamed x5, local copies, waits for them, and re-layouts  4.09 us

profile of v1, /device:TPU:1, one launch (start us, length us, event | category | flops | bytes accessed | tf_op | source)
XLA Modules:
  0.0 149.7 jit_solution(6071828334310412549)
XLA Ops:
  0.6 1.4 copy.11.ids_ref
  2.0 143.7 %shard_map.103 = (bf16[128,2048]{1,0:T(8,128)(2,1)}, bf16[128,2048]{1,0:T(8,128)(2,1)}, f32[8,128]{1,0:T(8,128)}) custom-call(bf16[128,2048]{1,0:T(8,128)(2,1)} %q_hbm.1, bf16[128,2048]{1,0:T(8,128)(2,1)} %k_hbm.1, bf16[128,2048]{1,0:T(8,128)(2,1)} %v_hbm.1, bf16[128,2048]{1,0:T(8,128)(2,1)} %mk_hbm.1, bf16[128,2048]{1,0:T(8,128)(2,1)} %mv_hbm.1, ...), custom_call_target="tpu_custom_call" | custom-call | tf_op jit(solution)/shard_map/pallas_call | solution.py:499
  145.7 1.2 slice_bitcast_fusion
  146.9 0.0 copy-start
  146.9 1.9 %copy.14 = bf16[128,2048]{1,0:T(8,128)(2,1)} copy(bf16[128,2048]{1,0:T(8,128)(2,1)} %get-tuple-element.12) | data formatting | bytes 1048576
  148.9 0.0 copy-done
  148.9 0.8 copy.15
Async XLA Ops:
  146.9 1.9 %copy-start = (bf16[128,2048]{1,0:T(8,128)(2,1)S(1)}, bf16[128,2048]{1,0:T(8,128)(2,1)}, u32[]{:S(2)}) copy-start(bf16[128,2048]{1,0:T(8,128)(2,1)} %get-tuple-element.13) | copy-start | bytes 1572868

commit v2 on v1

v2 whole, which is shorter than its diff:
```python
import functools
import math

import jax
import jax.numpy as jnp
from jax import lax
from jax.experimental import pallas as pl
from jax.experimental.pallas import tpu as pltpu
from jax.sharding import PartitionSpec as P

NX = 4
ROW = 2 * NX
HD = 128
QUARTER = 96
EIGHTH = QUARTER // 2
RING = NX * QUARTER
MESH = pl.DeviceIdType.MESH
F32 = jnp.float32
BF16 = jnp.bfloat16


def dot_nt(a, b):
    return lax.dot_general(a, b, (((1,), (1,)), ((), ())), preferred_element_type=F32)


def dot_nn(a, b):
    return jnp.dot(a, b, preferred_element_type=F32)


def row_sum(a):
    return jnp.sum(a, axis=-1, keepdims=True)


def kernel(
    nz, total_tokens,
    q_hbm, k_hbm, v_hbm, mk_hbm, mv_hbm, d_hbm, ids_ref, gl_ref,
    out_hbm, dq_hbm, gg_ref,
    kv, qs, gs, md, qg, mg, po, da, db, ls, dl,
    qh, kh, vh, dh, lo, ldq, lacc, rm, rq, so, sd, fo, fq, gx, codes, codes_sm, rr, ry, rz,
    loc, swap_s, swap_r,
    q_s, q_r, d_s, d_r, c_s, c_r, m_s, m_r, g_s, g_r,
    zk_s, zk_r, zv_s, zv_r,
    ya_s, ya_r, yb_s, yb_r, yc_s, yc_r, yd_s, yd_r,
    rr_s, rr_r, ry_s, ry_r, rz_s, rz_r,
):
    rows, width = q_hbm.shape
    wide = width // ROW
    mine_h = wide // HD
    heads = width // HD
    groups = ids_ref.shape[0]
    gr = rows // groups
    zrows = 4 * rows - RING
    scale = HD ** -0.5

    s = lax.axis_index("seq")
    m = lax.axis_index("mem")
    x, y = lax.rem(s, NX), s // NX
    z, c = m // 2, lax.rem(m, 2)
    r = x * 2 + c

    def at_row(step):
        p = lax.rem(r + step + ROW, ROW)
        return (y * NX + p // 2, z * 2 + lax.rem(p, 2))

    def at_y(step):
        return (lax.rem(y + step + NX, NX) * NX + x, m)

    def at_z(step):
        return (s, lax.rem(z + step + nz, nz) * 2 + c)

    sib = (s, z * 2 + 1 - c)

    def cols_of(p):
        return pl.ds(pl.multiple_of(p * wide, wide), wide)

    def rows_of(p):
        return pl.ds(pl.multiple_of(p * rows, rows), rows)

    own_k = kv.at[z, rows_of(c)]
    own_v = kv.at[z, rows_of(2 + c)]
    own = [
        pltpu.make_async_copy(src, dst, loc.at[i])
        for i, (src, dst) in enumerate((
            (mk_hbm.at[:, cols_of(r)], own_k),
            (mv_hbm.at[:, cols_of(r)], own_v),
            (q_hbm, qh),
            (k_hbm, kh),
            (v_hbm, vh),
            (d_hbm, dh),
            (q_hbm.at[:, cols_of(r)], qs.at[rows_of(r)]),
            (d_hbm.at[:, cols_of(r)], gs.at[rows_of(r)]),
        ))
    ]
    for cp in own:
        cp.start()

    barrier = pltpu.get_barrier_semaphore()

    def greet(dev):
        pl.semaphore_signal(barrier, inc=1, device_id=dev, device_id_type=MESH)

    for step in range(1, ROW):
        greet(at_row(step))
    for step in (1, -1):
        greet(at_y(step))
        greet(at_z(step))

    a0 = jnp.broadcast_to(ids_ref[:, 0:1], (groups, rows))
    a1 = jnp.broadcast_to(ids_ref[:, 1:2], (groups, rows))
    g_row = lax.broadcasted_iota(jnp.int32, (groups, rows), 0)
    g_tok = lax.broadcasted_iota(jnp.int32, (groups, rows), 1) // gr
    zero = jnp.zeros((groups, rows), jnp.int32)
    here = g_row == g_tok
    i0 = jnp.sum(jnp.where(here, a0, zero), axis=0, keepdims=True)
    i1 = jnp.sum(jnp.where(here, a1, zero), axis=0, keepdims=True)
    one = zero + 1
    earlier = g_row < g_tok
    r0 = jnp.sum(jnp.where(earlier & ((a0 == i0) | (a1 == i0)), one, zero), axis=0, keepdims=True)
    r1 = jnp.sum(jnp.where(earlier & ((a0 == i1) | (a1 == i1)), one, zero), axis=0, keepdims=True)
    code0 = i0 * (2 * ROW) + r * 2 + r0
    code1 = i1 * (2 * ROW) + r * 2 + r1
    first = lax.broadcasted_iota(jnp.int32, (8, rows), 0) == 0
    codes[r] = jnp.where(first, jnp.broadcast_to(code0, (8, rows)), jnp.broadcast_to(code1, (8, rows)))

    for j in range(heads):
        logit = jnp.full((8, HD), gl_ref[j], F32)
        gx[:, j * HD:(j + 1) * HD] = 1.0 / (1.0 + jnp.exp(-logit))

    pl.semaphore_wait(barrier, ROW - 1 + 4)

    swaps = [
        pltpu.make_async_remote_copy(
            src_ref=src.at[:, cols_of(x * 2 + 1 - c)], dst_ref=dst,
            send_sem=swap_s.at[i], recv_sem=swap_r.at[i], device_id=sib, device_id_type=MESH,
        )
        for i, (src, dst) in enumerate(((mk_hbm, own_k), (mv_hbm, own_v)))
    ]
    for cp in swaps:
        cp.start()

    def row_copy(src, dst, send, recv, step):
        return pltpu.make_async_remote_copy(
            src_ref=src, dst_ref=dst, send_sem=send.at[step], recv_sem=recv.at[step],
            device_id=at_row(step), device_id_type=MESH,
        )

    def to_row(step):
        p = lax.rem(r + step, ROW)
        return (
            row_copy(codes.at[r], codes.at[r], c_s, c_r, step),
            row_copy(q_hbm.at[:, cols_of(p)], qs.at[rows_of(r)], q_s, q_r, step),
            row_copy(d_hbm.at[:, cols_of(p)], gs.at[rows_of(r)], d_s, d_r, step),
        )

    def from_row(step):
        p = lax.rem(r + ROW - step, ROW)
        return (
            row_copy(codes.at[p], codes.at[p], c_s, c_r, step),
            row_copy(q_hbm.at[:, cols_of(p)], qs.at[rows_of(p)], q_s, q_r, step),
            row_copy(d_hbm.at[:, cols_of(p)], gs.at[rows_of(p)], d_s, d_r, step),
        )

    def push(o, row, count, send, recv, dev):
        here_ = kv.at[o, pl.ds(pl.multiple_of(row, 16), count)]
        return pltpu.make_async_remote_copy(
            src_ref=here_, dst_ref=here_, send_sem=send, recv_sem=recv, device_id=dev, device_id_type=MESH,
        )

    def k_z(o, j, step):
        return push(o, y * QUARTER, QUARTER, zk_s.at[j], zk_r.at[j], at_z(step))

    def v_z(o, j, step):
        return push(o, RING, zrows, zv_s.at[j], zv_r.at[j], at_z(step))

    def origin(n):
        away = (n + 1) // 2
        return lax.rem(z + nz + jnp.where(lax.rem(n, 2) == 1, -away, away), nz)

    last = nz - 1

    def forward_k(n, o):
        odd = lax.rem(n, 2) == 1

        @pl.when(odd & (n + 2 <= last))
        def _():
            k_z(o, n + 2, 1).start()

        @pl.when(jnp.logical_not(odd) & (n + 2 < last))
        def _():
            k_z(o, n + 2, -1).start()

    def forward_v(n, o):
        odd = lax.rem(n, 2) == 1

        @pl.when(odd & (n + 2 < last))
        def _():
            v_z(o, n + 2, 1).start()

        @pl.when(jnp.logical_not(odd) & (n + 1 <= last))
        def _():
            v_z(o, jnp.minimum(n + 2, last), -1).start()

    left = lax.rem(y + NX - 1, NX)
    right = lax.rem(y + 1, NX)
    far = lax.rem(y + 2, NX)

    def to_right(n, o):
        return push(o, y * QUARTER, QUARTER, ya_s.at[n], ya_r.at[n], at_y(1))

    def to_left(n, o):
        return push(o, y * QUARTER, QUARTER, yb_s.at[n], yb_r.at[n], at_y(-1))

    def from_left(n, o):
        return push(o, left * QUARTER, QUARTER, ya_s.at[n], ya_r.at[n], at_y(1))

    def from_right(n, o):
        return push(o, right * QUARTER, QUARTER, yb_s.at[n], yb_r.at[n], at_y(-1))

    def on_right(n, o):
        return push(o, left * QUARTER, EIGHTH, yc_s.at[n], yc_r.at[n], at_y(1))

    def on_left(n, o):
        return push(o, right * QUARTER + EIGHTH, EIGHTH, yd_s.at[n], yd_r.at[n], at_y(-1))

    def far_left(n, o):
        return push(o, far * QUARTER, EIGHTH, yc_s.at[n], yc_r.at[n], at_y(1))

    def far_right(n, o):
        return push(o, far * QUARTER + EIGHTH, EIGHTH, yd_s.at[n], yd_r.at[n], at_y(-1))

    def arrive(n):
        o = origin(n)
        k_z(o, n, 1).wait_recv()
        forward_k(n, o)
        to_right(n, o).start()
        to_left(n, o).start()
        v_z(o, n, 1).wait_recv()
        forward_v(n, o)

    def relay(n):
        o = origin(n)
        from_left(n, o).wait_recv()
        on_right(n, o).start()
        from_right(n, o).wait_recv()
        on_left(n, o).start()

    def settle(n):
        o = origin(n)
        far_left(n, o).wait_recv()
        far_right(n, o).wait_recv()

    def drain(n, carry):
        o = origin(n)
        for cp in (k_z(o, n, 1), v_z(o, n, 1), to_right(n, o), to_left(n, o), on_right(n, o), on_left(n, o)):
            cp.wait_send()
        return carry

    my_gate = gx.at[:, cols_of(r)]
    slots_b = 2 * ROW
    srows = slots_b * gr

    def attend(n):
        o = origin(n)
        units = [(blk, h) for blk in range(2) for h in range(mine_h)]
        for part in range(0, len(units), 4):
            todo = units[part:part + 4]
            kk, vv, sc, dp = [], [], [], []
            for blk, h in todo:
                cols = slice(h * HD, (h + 1) * HD)
                kk.append(kv[o, blk * rows:(blk + 1) * rows, cols])
                vv.append(kv[o, (2 + blk) * rows:(3 + blk) * rows, cols])
            for i, (blk, h) in enumerate(todo):
                cols = slice(h * HD, (h + 1) * HD)
                sc.append(dot_nt(qg[:, o * 2 + blk, :, cols].reshape(srows, HD), kk[i]) * scale)
            for i, (blk, h) in enumerate(todo):
                cols = slice(h * HD, (h + 1) * HD)
                dp.append(dot_nt(mg[:, o * 2 + blk, :, cols].reshape(srows, HD), vv[i]))
            peak = [jnp.max(a, axis=-1, keepdims=True) for a in sc]
            e = [jnp.exp(a - b) for a, b in zip(sc, peak)]
            tot = [row_sum(a) for a in e]
            p = [a * (1.0 / b) for a, b in zip(e, tot)]
            pb = [a.astype(BF16) for a in p]
            delta = [row_sum(a * b) for a, b in zip(p, dp)]
            dsb = [(a * (b - d)).astype(BF16) for a, b, d in zip(p, dp, delta)]
            for i, (blk, h) in enumerate(todo):
                cols = slice(h * HD, (h + 1) * HD)
                sl = pl.ds((o * 2 + blk) * slots_b, slots_b)
                cube = (slots_b, gr, HD)
                po[sl, :, cols] = dot_nn(pb[i], vv[i]).reshape(cube)
                db[sl, :, cols] = dot_nn(pb[i], kk[i]).reshape(cube)
                da[sl, :, cols] = dot_nn(dsb[i], kk[i]).reshape(cube)
                ls[sl, :, cols] = jnp.broadcast_to(peak[i] + jnp.log(tot[i]), (srows, HD)).reshape(cube)
                dl[sl, :, cols] = jnp.broadcast_to(delta[i], (srows, HD)).reshape(cube)

    def pick(d, carry):
        here_ = rows_of(d)
        md[here_, :] = (my_gate[0:1, :] * gs[here_, :].astype(F32)).astype(BF16)
        lane = lax.broadcasted_iota(jnp.int32, (1, rows), 1) & (gr - 1)
        c0, c1 = codes[d, 0:1, :], codes[d, 1:2, :]
        t0 = ((c0 // (2 * ROW)) * 2 + (c0 & 1)) * gr + lane
        t1 = ((c1 // (2 * ROW)) * 2 + (c1 & 1)) * gr + lane
        count = qg.shape[1] * 2 * gr
        at = lax.broadcasted_iota(jnp.int32, (count, rows), 0)
        hot = jnp.where((at == t0) | (at == t1), 1.0, 0.0).astype(BF16)
        cube = (qg.shape[1], 2 * gr, wide)
        qg[d] = dot_nn(hot, qs[here_, :]).astype(BF16).reshape(cube)
        mg[d] = dot_nn(hot, md[here_, :]).astype(BF16).reshape(cube)
        return carry

    ahead = 4

    def local(i):
        ri = lax.broadcasted_iota(jnp.int32, (rows, rows), 0)
        ci = lax.broadcasted_iota(jnp.int32, (rows, rows), 1)
        cols = [pl.ds(pl.multiple_of(i * (ahead * HD) + h * HD, HD), HD) for h in range(ahead)]
        kk = [kh[:, a] for a in cols]
        vv = [vh[:, a] for a in cols]
        g = [dh[:, a].astype(F32) for a in cols]
        ld = [((1.0 - gx[0:1, a]) * b).astype(BF16) for a, b in zip(cols, g)]
        sc = [jnp.where(ri >= ci, dot_nt(qh[:, a], b) * scale, -1e30) for a, b in zip(cols, kk)]
        dp = [dot_nt(a, b) for a, b in zip(ld, vv)]
        e = [jnp.exp(a - jnp.max(a, axis=-1, keepdims=True)) for a in sc]
        p = [a * (1.0 / row_sum(a)) for a in e]
        o = [dot_nn(a.astype(BF16), b) for a, b in zip(p, vv)]
        delta = [row_sum(a.astype(F32) * b) for a, b in zip(ld, o)]
        ds = [(a * (b - d)).astype(BF16) for a, b, d in zip(p, dp, delta)]
        for h, a in enumerate(cols):
            lo[:, a] = o[h]
            ldq[:, a] = dot_nn(ds[h], kk[h]) * scale
            lacc[:, a] = jnp.sum((g[h] * o[h]).reshape(rows // 8, 8, HD), axis=0)

    own[0].wait()
    swap_in = [
        pltpu.make_async_remote_copy(
            src_ref=src.at[:, cols_of(r)], dst_ref=kv.at[z, rows_of(base + 1 - c)],
            send_sem=swap_s.at[i], recv_sem=swap_r.at[i], device_id=sib, device_id_type=MESH,
        )
        for i, (src, base) in enumerate(((mk_hbm, 0), (mv_hbm, 2)))
    ]
    own[1].wait()
    swap_in[0].wait_recv()
    swap_in[1].wait_recv()
    k_z(z, 1, 1).start()
    k_z(z, 2, -1).start()
    v_z(z, 1, 1).start()
    v_z(z, 2, -1).start()

    def send_row(step, carry):
        for cp in to_row(step):
            cp.start()
        return carry

    lax.fori_loop(1, ROW, send_row, 0)
    for cp in own[2:]:
        cp.wait()

    relay_lag, settle_lag, ready = 2, 4, 9

    def turn(n, carry):
        @pl.when(n <= last)
        def _():
            arrive(n)

        @pl.when((n > relay_lag) & (n - relay_lag <= last))
        def _():
            relay(n - relay_lag)

        @pl.when(n > settle_lag)
        def _():
            settle(n - settle_lag)

        @pl.when(n <= heads // ahead)
        def _():
            local(n - 1)

        @pl.when(n == ready)
        def _():
            def take(step, carry):
                for cp in from_row(step):
                    cp.wait_recv()
                return carry

            lax.fori_loop(1, ROW, take, 0)
            lax.fori_loop(0, ROW, pick, 0)
            to_smem = pltpu.make_async_copy(codes, codes_sm, loc.at[8])
            to_smem.start()
            to_smem.wait()

        def reached(t):
            return jnp.maximum(jnp.minimum(t - settle_lag + 1, 2 * (t - ready + 1)), 0)

        def step(i, carry):
            attend(i)
            return carry

        lax.fori_loop(reached(n - 1), reached(n), step, 0)
        return carry

    lax.fori_loop(1, last + settle_lag + 1, turn, 0)

    def blend(base, g, at, second):
        d0, d1 = codes_sm[base, 0, g * gr], codes_sm[base, 1, g * gr]
        l0, l1 = ls[d0], ls[d1]
        peak = jnp.maximum(l0, l1)
        e0, e1 = jnp.exp(l0 - peak), jnp.exp(l1 - peak)
        inv = 1.0 / (e0 + e1)
        s0, s1 = e0 * inv, e1 * inv
        mo = s0 * po[d0] + s1 * po[d1]
        own_rows = slice(gr, 2 * gr) if second else slice(0, gr)
        prod = md[at, :].astype(F32)[own_rows] * mo
        delta = jnp.concatenate(
            [jnp.broadcast_to(row_sum(prod[:, h * HD:(h + 1) * HD]), (gr, HD)) for h in range(mine_h)], axis=1
        )
        dq = s0 * (da[d0] + (dl[d0] - delta) * db[d0])
        dq = dq + s1 * (da[d1] + (dl[d1] - delta) * db[d1])
        return mo, dq * scale

    def give_back(p, step):
        return (
            row_copy(so.at[rows_of(p)], rm.at[:, cols_of(r)], m_s, m_r, step),
            row_copy(sd.at[rows_of(p)], rq.at[:, cols_of(r)], g_s, g_r, step),
        )

    def merge(i, acc):
        step = lax.rem(i + ROW // 2, ROW)
        base = lax.rem(r + step, ROW)

        def pair(g2, acc):
            g = g2 * 2
            at = pl.ds(pl.multiple_of(base * rows + g * gr, 2 * gr), 2 * gr)
            ma, qa = blend(base, g, at, False)
            mb, qb = blend(base, g + 1, at, True)
            mo = jnp.concatenate([ma, mb], axis=0)
            so[at, :] = mo.astype(BF16)
            sd[at, :] = jnp.concatenate([qa, qb], axis=0).astype(BF16)
            t = gs[at, :].astype(F32) * mo
            return acc + t[:gr] + t[gr:]

        acc = lax.fori_loop(0, groups // 2, pair, acc)

        @pl.when(step > 0)
        def _():
            for cp in give_back(base, step):
                cp.start()

        @pl.when(step == 0)
        def _():
            pltpu.make_async_copy(so.at[rows_of(r)], rm.at[:, cols_of(r)], loc.at[9]).start()
            pltpu.make_async_copy(sd.at[rows_of(r)], rq.at[:, cols_of(r)], loc.at[10]).start()

        return acc

    acc = lax.fori_loop(0, ROW, merge, jnp.zeros((gr, wide), F32))

    lane = lax.broadcasted_iota(jnp.int32, (8, HD), 1)
    term = jnp.zeros((8, HD), F32)
    gates = jnp.zeros((8, HD), F32)

    def spread(a):
        return jnp.broadcast_to(jnp.sum(row_sum(a), axis=0, keepdims=True), (8, HD))

    for j in range(heads):
        cols = slice(j * HD, (j + 1) * HD)
        term = jnp.where(lane == j, -spread(lacc[:, cols]), term)
        gates = jnp.where(lane == j, gx[:, cols], gates)
    for j in range(mine_h):
        term = term + jnp.where(lane == r * mine_h + j, spread(acc[:, j * HD:(j + 1) * HD]), 0.0)
    term = term * gates * (1.0 - gates) * (1.0 / math.sqrt(total_tokens))

    def exchange(buf, place, at, send, recv):
        size = buf.shape[0]

        def make(step, src):
            return pltpu.make_async_remote_copy(
                src_ref=buf.at[src], dst_ref=buf.at[src], send_sem=send.at[step], recv_sem=recv.at[step],
                device_id=at(step), device_id_type=MESH,
            )

        def start(step, carry):
            make(step, place).start()
            return carry

        def wait(step, carry):
            make(step, lax.rem(place + size - step, size)).wait_recv()
            make(step, place).wait_send()
            return carry

        lax.fori_loop(1, size, start, 0)
        lax.fori_loop(1, size, wait, 0)
        out = buf[0]
        for i in range(1, size):
            out = out + buf[i]
        return out

    rr[r] = term
    term = exchange(rr, r, at_row, rr_s, rr_r)
    ry[y] = term
    term = exchange(ry, y, at_y, ry_s, ry_r)
    rz[z] = term
    gg_ref[...] = exchange(rz, z, at_z, rz_s, rz_r)

    def taken(step, carry):
        for cp in give_back(r, step):
            cp.wait_send()
        p = lax.rem(r + ROW - step, ROW)
        row_copy(so.at[rows_of(r)], rm.at[:, cols_of(p)], m_s, m_r, step).wait_recv()
        row_copy(sd.at[rows_of(r)], rq.at[:, cols_of(p)], g_s, g_r, step).wait_recv()
        return carry

    lax.fori_loop(1, ROW, taken, 0)
    pltpu.make_async_copy(so.at[rows_of(r)], rm.at[:, cols_of(r)], loc.at[9]).wait()
    pltpu.make_async_copy(sd.at[rows_of(r)], rq.at[:, cols_of(r)], loc.at[10]).wait()

    def finish(i, carry):
        at = pl.ds(pl.multiple_of(i * 16, 16), 16)
        gate = gx[0:1, :]
        fo[at, :] = (gate * rm[at, :].astype(F32) + (1.0 - gate) * lo[at, :]).astype(BF16)
        fq[at, :] = (ldq[at, :] + rq[at, :].astype(F32)).astype(BF16)
        return carry

    lax.fori_loop(0, rows // 16, finish, 0)
    keep = [
        pltpu.make_async_copy(fo, out_hbm, loc.at[0]),
        pltpu.make_async_copy(fq, dq_hbm, loc.at[1]),
    ]
    for cp in keep:
        cp.start()

    for cp in swaps:
        cp.wait_send()

    def sent(step, carry):
        for cp in to_row(step):
            cp.wait_send()
        return carry

    lax.fori_loop(1, ROW, sent, 0)
    lax.fori_loop(1, nz, drain, 0)
    for cp in keep:
        cp.wait()


def body(total_tokens, query, key, value, mem_key, mem_value, block_ids, gate_logit, d_out):
    rows, width = query.shape
    wide = width // ROW
    nz = lax.axis_size("mem") // 2
    gr = rows // block_ids.shape[0]
    blocks = 2 * nz
    dma = pltpu.SemaphoreType.DMA
    any_ = pl.BlockSpec(memory_space=pl.ANY)
    vmem = pl.BlockSpec(memory_space=pltpu.VMEM)
    smem = pl.BlockSpec(memory_space=pltpu.SMEM)
    heads = width // HD
    scratch = (
        [pltpu.VMEM((nz, 4 * rows, wide), BF16)]
        + [pltpu.VMEM((ROW * rows, wide), BF16)] * 3
        + [pltpu.VMEM((ROW, blocks, 2 * gr, wide), BF16)] * 2
        + [pltpu.VMEM((blocks * 2 * ROW, gr, wide), F32)] * 5
        + [pltpu.VMEM((rows, width), BF16)] * 4
        + [pltpu.VMEM((rows, width), F32)] * 2
        + [pltpu.VMEM((8, width), F32)]
        + [pltpu.VMEM((rows, width), BF16)] * 2
        + [pltpu.VMEM((ROW * rows, wide), BF16)] * 2
        + [pltpu.VMEM((rows, width), BF16)] * 2
        + [pltpu.VMEM((8, width), F32)]
        + [pltpu.VMEM((ROW, 8, rows), jnp.int32), pltpu.SMEM((ROW, 8, rows), jnp.int32)]
        + [pltpu.VMEM((size, 8, HD), F32) for size in (ROW, NX, nz)]
        + [dma((11,)), dma((2,)), dma((2,))]
        + [dma((ROW,))] * 10
        + [dma((nz,))] * 12
        + [dma((size,)) for size in (ROW, ROW, NX, NX, nz, nz)]
    )
    out, d_query, gate = pl.pallas_call(
        functools.partial(kernel, nz, total_tokens),
        out_shape=(
            jax.ShapeDtypeStruct((rows, width), BF16),
            jax.ShapeDtypeStruct((rows, width), BF16),
            jax.ShapeDtypeStruct((8, HD), F32),
        ),
        in_specs=[any_] * 6 + [vmem, smem],
        out_specs=(any_, any_, vmem),
        scratch_shapes=scratch,
        compiler_params=pltpu.CompilerParams(
            collective_id=0, has_side_effects=True, vmem_limit_bytes=56 * 1024 * 1024
        ),
    )(query, key, value, mem_key, mem_value, d_out, block_ids, gate_logit)
    return out, d_query, gate[0, :heads]


def solution(mesh):
    tokens = P(("seq", "mem"), None)

    def run(query, *rest):
        return jax.shard_map(
            functools.partial(body, query.shape[0]),
            mesh=mesh,
            in_specs=(tokens, tokens, tokens, P("mem", None), P("mem", None), tokens, P(), tokens),
            out_specs=(tokens, tokens, P()),
            check_vma=False,
        )(query, *rest)

    return run
```

time: 150 us -> 94.2 us (0.63)
  Pallas kernels: 144 us -> 87.5 us
    pallas_call x1, Pallas kernels: 144 us -> 87.5 us  [body(): pl.pallas_call(functools.partial(kernel, nz, total_tokens), out_shape=(ja...]
where the time goes in v2:
time: 94.2 us; the launch traced here: 93.5 us
  Pallas kernels  87.5 us (93%)
  local copies, waits for them, and re-layouts  5.27 us (6%)
    pallas_call x1, Pallas kernels, body(): pl.pallas_call(functools.partial(kernel, nz, total_tokens), out_shape=(ja...  87.5 us
    unnamed x5, local copies, waits for them, and re-layouts  4.09 us

profile of v2, /device:TPU:1, one launch (start us, length us, event | category | flops | bytes accessed | tf_op | source)
XLA Modules:
  0.0 93.5 jit_solution(10718829821397674077)
XLA Ops:
  0.6 1.4 %copy.11.ids_ref = s32[16,2]{1,0:T(8,128)} copy(s32[16,2]{0,1:T(2,128)} %param.13) | data formatting | bytes 256 | tf_op args[5]
  2.0 87.5 %shard_map.103 = (bf16[128,2048]{1,0:T(8,128)(2,1)}, bf16[128,2048]{1,0:T(8,128)(2,1)}, f32[8,128]{1,0:T(8,128)}) custom-call(bf16[128,2048]{1,0:T(8,128)(2,1)} %q_hbm.1, bf16[128,2048]{1,0:T(8,128)(2,1)} %k_hbm.1, bf16[128,2048]{1,0:T(8,128)(2,1)} %v_hbm.1, bf16[128,2048]{1,0:T(8,128)(2,1)} %mk_hbm.1, bf16[128,2048]{1,0:T(8,128)(2,1)} %mv_hbm.1, ...), custom_call_target="tpu_custom_call" | custom-call | tf_op jit(solution)/shard_map/pallas_call | solution.py:573
  89.5 1.2 %slice_bitcast_fusion = f32[16]{0:T(128)} fusion(f32[8,128]{1,0:T(8,128)} %get-tuple-element.8), kind=kLoop, calls=%fused_computation | loop fusion | bytes 128 | tf_op jit(solution)/shard_map/squeeze | solution.py:587
  90.7 0.0 copy-start
  90.7 1.9 %copy.14 = bf16[128,2048]{1,0:T(8,128)(2,1)} copy(bf16[128,2048]{1,0:T(8,128)(2,1)} %get-tuple-element.12) | data formatting | bytes 1048576
  92.7 0.0 copy-done
  92.7 0.8 copy.15
Async XLA Ops:
  90.7 1.9 %copy-start = (bf16[128,2048]{1,0:T(8,128)(2,1)S(1)}, bf16[128,2048]{1,0:T(8,128)(2,1)}, u32[]{:S(2)}) copy-start(bf16[128,2048]{1,0:T(8,128)(2,1)} %get-tuple-element.13) | copy-start | bytes 1572868

commit v3 on v2

v3 whole, which is shorter than its diff:
```python
import functools
import math

import jax
import jax.numpy as jnp
from jax import lax
from jax.experimental import pallas as pl
from jax.experimental.pallas import tpu as pltpu
from jax.sharding import PartitionSpec as P

HD = 128
MESH = pl.DeviceIdType.MESH
F32 = jnp.float32
BF16 = jnp.bfloat16


def dot_nt(a, b):
    return lax.dot_general(a, b, (((1,), (1,)), ((), ())), preferred_element_type=F32)


def dot_nn(a, b):
    return jnp.dot(a, b, preferred_element_type=F32)


def row_sum(a):
    return jnp.sum(a, axis=-1, keepdims=True)


def kernel(
    nz, total_tokens,
    q_hbm, k_hbm, v_hbm, mk_hbm, mv_hbm, d_hbm, ids_ref, gl_ref,
    rm, rq, lo_hbm, ldq_hbm, gg_ref,
    kv, qs, gs, md, qg, po, da, db, ls, dl,
    qh, kh, vh, dh, lo, ldq, lacc, so, sd, gx, codes, codes_sm, rr, ry, rz,
    loc,
    q_s, q_r, d_s, d_r, c_s, c_r, m_s, m_r, g_s, g_r,
    z_s, z_r, b_s, b_r,
    rr_s, rr_r, ry_s, ry_r, rz_s, rz_r,
):
    rows, width = q_hbm.shape
    heads = width // HD
    plane = qg.shape[0]
    groups = ids_ref.shape[1]
    gr = rows // groups
    scale = HD ** -0.5

    s = lax.axis_index("seq")
    m = lax.axis_index("mem")
    z, c = m // 2, lax.rem(m, 2)
    toward = 1 - 2 * c

    def at_plane(step):
        return (lax.rem(s + step, plane), m)

    def at_z(step):
        return (s, lax.rem(z + step + nz, nz) * 2 + c)

    def at_sib(step):
        return (s, z * 2 + 1 - c)

    sib = at_sib(1)

    def cols_of(p):
        return pl.ds(pl.multiple_of(p * HD, HD), HD)

    def rows_of(p):
        return pl.ds(pl.multiple_of(p * rows, rows), rows)

    own = [
        pltpu.make_async_copy(src, dst, loc.at[i])
        for i, (src, dst) in enumerate((
            (mk_hbm.at[:, cols_of(s)], kv.at[z, c, 0]),
            (mv_hbm.at[:, cols_of(s)], kv.at[z, c, 1]),
            (q_hbm, qh),
            (d_hbm, dh),
            (k_hbm, kh),
            (v_hbm, vh),
        ))
    ]
    for cp in own:
        cp.start()

    barrier = pltpu.get_barrier_semaphore()

    def greet(dev):
        pl.semaphore_signal(barrier, inc=1, device_id=dev, device_id_type=MESH)

    greet(sib)
    for step in (1, -1, 2, -2):
        greet(at_z(step))

    def greet_plane(step, carry):
        greet(at_plane(step))
        return carry

    lax.fori_loop(1, plane, greet_plane, 0)

    g_row = lax.broadcasted_iota(jnp.int32, (groups, rows), 0)
    g_tok = lax.broadcasted_iota(jnp.int32, (groups, rows), 1) // gr
    zero = jnp.zeros((groups, rows), jnp.int32)
    a0, a1, i0, i1 = zero, zero, zero, zero
    for g in range(groups):
        b0, b1 = ids_ref[0, g], ids_ref[1, g]
        a0, a1 = jnp.where(g_row == g, b0, a0), jnp.where(g_row == g, b1, a1)
        i0, i1 = jnp.where(g_tok == g, b0, i0), jnp.where(g_tok == g, b1, i1)
    one = zero + 1
    earlier = g_row < g_tok
    r0 = jnp.sum(jnp.where(earlier & ((a0 == i0) | (a1 == i0)), one, zero), axis=0, keepdims=True)
    r1 = jnp.sum(jnp.where(earlier & ((a0 == i1) | (a1 == i1)), one, zero), axis=0, keepdims=True)
    code0 = i0[0:1] * (2 * plane) + s * 2 + r0
    code1 = i1[0:1] * (2 * plane) + s * 2 + r1
    first = lax.broadcasted_iota(jnp.int32, (8, rows), 0) == 0
    codes[s] = jnp.where(first, jnp.broadcast_to(code0, (8, rows)), jnp.broadcast_to(code1, (8, rows)))

    for j in range(heads):
        logit = jnp.full((8, HD), gl_ref[j], F32)
        gx[:, j * HD:(j + 1) * HD] = 1.0 / (1.0 + jnp.exp(-logit))

    pl.semaphore_wait(barrier, plane - 1 + 5)

    def plane_copy(src, dst, send, recv, step):
        return pltpu.make_async_remote_copy(
            src_ref=src, dst_ref=dst, send_sem=send.at[step], recv_sem=recv.at[step],
            device_id=at_plane(step), device_id_type=MESH,
        )

    def to_plane(step):
        p = lax.rem(s + step, plane)
        return (
            plane_copy(codes.at[s], codes.at[s], c_s, c_r, step),
            plane_copy(qh.at[:, cols_of(p)], qs.at[rows_of(s)], q_s, q_r, step),
            plane_copy(dh.at[:, cols_of(p)], gs.at[rows_of(s)], d_s, d_r, step),
        )

    def from_plane(step):
        p = lax.rem(s + plane - step, plane)
        return (
            plane_copy(codes.at[p], codes.at[p], c_s, c_r, step),
            plane_copy(qh.at[:, cols_of(p)], qs.at[rows_of(p)], q_s, q_r, step),
            plane_copy(dh.at[:, cols_of(p)], gs.at[rows_of(p)], d_s, d_r, step),
        )

    last = nz - 1

    def origin(n):
        away = (n + 1) // 2 * toward
        return lax.rem(z + nz + jnp.where(lax.rem(n, 2) == 1, -away, away), nz)

    def along_z(o, n, step):
        return pltpu.make_async_remote_copy(
            src_ref=kv.at[o, c], dst_ref=kv.at[o, c], send_sem=z_s.at[n], recv_sem=z_r.at[n],
            device_id=at_z(step), device_id_type=MESH,
        )

    def across(o, who):
        return pltpu.make_async_remote_copy(
            src_ref=kv.at[o, who], dst_ref=kv.at[o, who], send_sem=b_s.at[o], recv_sem=b_r.at[o],
            device_id=sib, device_id_type=MESH,
        )

    def spread_z(o, hops):
        @pl.when(2 * hops + 3 <= last)
        def _():
            along_z(o[0], 2 * hops + 3, 2 * toward).start()

        @pl.when(2 * hops + 4 <= last)
        def _():
            along_z(o[1], 2 * hops + 4, -2 * toward).start()

        along_z(o[0], 2 * hops + 1, toward).start()
        along_z(o[1], 2 * hops + 2, -toward).start()

    def arrive(n):
        o = origin(n)
        along_z(o, n, 1).wait_recv()
        across(o, c).start()

    def drain(n, carry):
        along_z(z, n, 1).wait_send()
        across(origin(n), c).wait_send()
        return carry

    my_gate = gx.at[:, cols_of(s)]
    slots_b = 2 * plane
    srows = slots_b * gr

    def attend(n):
        o = origin(n)
        todo = range(2)
        at = [qg.at[:, o * 2 + blk] for blk in todo]
        kk = [kv[o, blk, 0] for blk in todo]
        vv = [kv[o, blk, 1] for blk in todo]
        sc = [dot_nt(at[i][:, :, 0:HD].reshape(srows, HD), kk[i]) * scale for i in todo]
        dp = [dot_nt(at[i][:, :, HD:2 * HD].reshape(srows, HD), vv[i]) for i in todo]
        peak = [jnp.max(a, axis=-1, keepdims=True) for a in sc]
        e = [jnp.exp(a - b) for a, b in zip(sc, peak)]
        tot = [row_sum(a) for a in e]
        p = [a * (1.0 / b) for a, b in zip(e, tot)]
        pb = [a.astype(BF16) for a in p]
        delta = [row_sum(a * b) for a, b in zip(p, dp)]
        dsb = [(a * (b - d)).astype(BF16) for a, b, d in zip(p, dp, delta)]
        cube = (slots_b, gr, HD)
        for i in todo:
            sl = pl.ds((o * 2 + i) * slots_b, slots_b)
            po[sl] = dot_nn(pb[i], vv[i]).reshape(cube)
            db[sl] = dot_nn(pb[i], kk[i]).reshape(cube)
            da[sl] = dot_nn(dsb[i], kk[i]).reshape(cube)
            ls[sl] = jnp.broadcast_to(peak[i] + jnp.log(tot[i]), (srows, HD)).reshape(cube)
            dl[sl] = jnp.broadcast_to(delta[i], (srows, HD)).reshape(cube)

    def pick(d, carry):
        here_ = rows_of(d)
        md[here_, :] = (my_gate[0:1, :] * gs[here_, :].astype(F32)).astype(BF16)
        lane = lax.broadcasted_iota(jnp.int32, (1, rows), 1) & (gr - 1)
        c0, c1 = codes[d, 0:1, :], codes[d, 1:2, :]
        t0 = ((c0 // (2 * plane)) * 2 + (c0 & 1)) * gr + lane
        t1 = ((c1 // (2 * plane)) * 2 + (c1 & 1)) * gr + lane
        count = qg.shape[1] * 2 * gr
        at = lax.broadcasted_iota(jnp.int32, (count, rows), 0)
        hot = jnp.where((at == t0) | (at == t1), 1.0, 0.0).astype(BF16)
        both = jnp.concatenate([qs[here_, :], md[here_, :]], axis=1)
        qg[d] = dot_nn(hot, both).astype(BF16).reshape(qg.shape[1], 2 * gr, 2 * HD)
        return carry

    ahead = 4

    def local(i):
        ri = lax.broadcasted_iota(jnp.int32, (rows, rows), 0)
        ci = lax.broadcasted_iota(jnp.int32, (rows, rows), 1)
        cols = [pl.ds(pl.multiple_of(i * (ahead * HD) + h * HD, HD), HD) for h in range(ahead)]
        kk = [kh[:, a] for a in cols]
        vv = [vh[:, a] for a in cols]
        g = [dh[:, a].astype(F32) for a in cols]
        ld = [((1.0 - gx[0:1, a]) * b).astype(BF16) for a, b in zip(cols, g)]
        sc = [jnp.where(ri >= ci, dot_nt(qh[:, a], b) * scale, -1e30) for a, b in zip(cols, kk)]
        dp = [dot_nt(a, b) for a, b in zip(ld, vv)]
        e = [jnp.exp(a - jnp.max(a, axis=-1, keepdims=True)) for a in sc]
        p = [a * (1.0 / row_sum(a)) for a in e]
        o = [dot_nn(a.astype(BF16), b) for a, b in zip(p, vv)]
        delta = [row_sum(a.astype(F32) * b) for a, b in zip(ld, o)]
        ds = [(a * (b - d)).astype(BF16) for a, b, d in zip(p, dp, delta)]
        for h, a in enumerate(cols):
            lo[:, a] = (1.0 - gx[0:1, a]) * o[h]
            ldq[:, a] = dot_nn(ds[h], kk[h]) * scale
            lacc[:, a] = jnp.sum((g[h] * o[h]).reshape(rows // 8, 8, HD), axis=0)

    home = [
        pltpu.make_async_copy(lo, lo_hbm, loc.at[0]),
        pltpu.make_async_copy(ldq, ldq_hbm, loc.at[1]),
    ]

    own[0].wait()
    own[1].wait()
    spread_z((z, z), 0)
    across(z, c).start()
    own[2].wait()
    own[3].wait()

    def send_plane(step, carry):
        for cp in to_plane(step):
            cp.start()
        return carry

    lax.fori_loop(1, plane, send_plane, 0)
    keep = [
        pltpu.make_async_copy(qh.at[:, cols_of(s)], qs.at[rows_of(s)], loc.at[6]),
        pltpu.make_async_copy(dh.at[:, cols_of(s)], gs.at[rows_of(s)], loc.at[7]),
    ]
    for cp in keep:
        cp.start()
    own[4].wait()
    own[5].wait()

    turns = nz // 4
    ready = 3

    def turn(t, carry):
        far = 4 * t - 1

        @pl.when(t < turns)
        def _():
            a, b = origin(far), origin(far + 1)
            along_z(a, far, 1).wait_recv()
            along_z(b, far + 1, 1).wait_recv()
            spread_z((a, b), 2 * t)
            across(a, c).start()
            across(b, c).start()

        @pl.when(t <= turns)
        def _():
            arrive(far - 2)
            arrive(far - 1)

        @pl.when(t == turns)
        def _():
            arrive(far)

        @pl.when(t <= 2)
        def _():
            local(2 * t - 2)
            local(2 * t - 1)

        @pl.when(t == 2)
        def _():
            for cp in home:
                cp.start()

        @pl.when(t == ready)
        def _():
            def take(step, carry):
                for cp in from_plane(step):
                    cp.wait_recv()
                return carry

            lax.fori_loop(1, plane, take, 0)
            for cp in keep:
                cp.wait()
            lax.fori_loop(0, plane, pick, 0)
            to_smem = pltpu.make_async_copy(codes, codes_sm, loc.at[8])
            to_smem.start()
            to_smem.wait()

        def reached(t):
            return jnp.maximum(jnp.minimum(jnp.minimum(4 * t - 2, nz), 7 * (t - ready + 1)), 0)

        def step(i, carry):
            across(origin(i), 1 - c).wait_recv()
            attend(i)
            return carry

        lax.fori_loop(reached(t - 1), reached(t), step, 0)
        return carry

    lax.fori_loop(1, turns + 2, turn, 0)

    def blend(base, g0, count):
        rows_ = pl.ds(pl.multiple_of(base * rows + g0 * gr, 2 * gr), count * gr)
        gs_ = [g0 + i for i in range(count)]
        d0 = [codes_sm[base, 0, g * gr] for g in gs_]
        d1 = [codes_sm[base, 1, g * gr] for g in gs_]
        l0, l1 = [ls[d] for d in d0], [ls[d] for d in d1]
        peak = [jnp.maximum(a, b) for a, b in zip(l0, l1)]
        e0 = [jnp.exp(a - b) for a, b in zip(l0, peak)]
        e1 = [jnp.exp(a - b) for a, b in zip(l1, peak)]
        inv = [1.0 / (a + b) for a, b in zip(e0, e1)]
        s0 = [a * b for a, b in zip(e0, inv)]
        s1 = [a * b for a, b in zip(e1, inv)]
        mo = [a * po[i] + b * po[j] for a, b, i, j in zip(s0, s1, d0, d1)]
        grads = md[rows_, :].astype(F32)
        prod = [grads[i * gr:(i + 1) * gr] * a for i, a in enumerate(mo)]
        delta = [row_sum(a) for a in prod]
        dq = [a * (da[i] + (dl[i] - d) * db[i]) for a, i, d in zip(s0, d0, delta)]
        dq = [q + a * (da[i] + (dl[i] - d) * db[i]) for q, a, i, d in zip(dq, s1, d1, delta)]
        so[rows_, :] = (my_gate[0:1, :] * jnp.concatenate(mo, axis=0)).astype(BF16)
        sd[rows_, :] = (scale * jnp.concatenate(dq, axis=0)).astype(BF16)
        draw = gs[rows_, :].astype(F32)
        return sum([draw[i * gr:(i + 1) * gr] * a for i, a in enumerate(mo)])

    def give_back(p, step):
        return (
            plane_copy(so.at[rows_of(p)], rm.at[:, cols_of(s)], m_s, m_r, step),
            plane_copy(sd.at[rows_of(p)], rq.at[:, cols_of(s)], g_s, g_r, step),
        )

    own_back = [
        pltpu.make_async_copy(so.at[rows_of(s)], rm.at[:, cols_of(s)], loc.at[9]),
        pltpu.make_async_copy(sd.at[rows_of(s)], rq.at[:, cols_of(s)], loc.at[10]),
    ]
    together = 16

    def merge(i, acc):
        step = lax.rem(i + plane // 2, plane)
        base = lax.rem(s + step, plane)

        def some(i, acc):
            return acc + blend(base, i * together, together)

        acc = lax.fori_loop(0, groups // together, some, acc)

        @pl.when(step > 0)
        def _():
            for cp in give_back(base, step):
                cp.start()

        @pl.when(step == 0)
        def _():
            for cp in own_back:
                cp.start()

        return acc

    acc = lax.fori_loop(0, plane, merge, jnp.zeros((gr, HD), F32))

    lane = lax.broadcasted_iota(jnp.int32, (8, HD), 1)
    term = jnp.zeros((8, HD), F32)
    gates = jnp.zeros((8, HD), F32)

    def spread(a):
        return jnp.broadcast_to(jnp.sum(row_sum(a), axis=0, keepdims=True), (8, HD))

    for j in range(heads):
        cols = slice(j * HD, (j + 1) * HD)
        term = jnp.where(lane == j, -spread(lacc[:, cols]), term)
        gates = jnp.where(lane == j, gx[:, cols], gates)
    term = term + jnp.where(lane == s, spread(acc), 0.0)
    term = term * gates * (1.0 - gates) * (1.0 / math.sqrt(total_tokens))

    def exchange(buf, place, at, send, recv):
        size = buf.shape[0]

        def make(step, src):
            return pltpu.make_async_remote_copy(
                src_ref=buf.at[src], dst_ref=buf.at[src], send_sem=send.at[step], recv_sem=recv.at[step],
                device_id=at(step), device_id_type=MESH,
            )

        def start(step, carry):
            make(step, place).start()
            return carry

        def wait(step, carry):
            make(step, lax.rem(place + size - step, size)).wait_recv()
            make(step, place).wait_send()
            return carry

        lax.fori_loop(1, size, start, 0)
        lax.fori_loop(1, size, wait, 0)
        out = buf[0]
        for i in range(1, size):
            out = out + buf[i]
        return out

    rz[z] = term
    term = exchange(rz, z, at_z, rz_s, rz_r)
    ry[c] = term
    term = exchange(ry, c, at_sib, ry_s, ry_r)
    rr[s] = term
    gg_ref[...] = exchange(rr, s, at_plane, rr_s, rr_r)

    def taken(step, carry):
        p = lax.rem(s + plane - step, plane)
        for cp in give_back(s, step):
            cp.wait_send()
        plane_copy(so.at[rows_of(s)], rm.at[:, cols_of(p)], m_s, m_r, step).wait_recv()
        plane_copy(sd.at[rows_of(s)], rq.at[:, cols_of(p)], g_s, g_r, step).wait_recv()
        return carry

    lax.fori_loop(1, plane, taken, 0)
    for cp in own_back:
        cp.wait()

    def sent(step, carry):
        for cp in to_plane(step):
            cp.wait_send()
        return carry

    lax.fori_loop(1, plane, sent, 0)
    across(z, c).wait_send()
    lax.fori_loop(1, nz, drain, 0)
    for cp in home:
        cp.wait()


def body(total_tokens, query, key, value, mem_key, mem_value, block_ids, gate_logit, d_out):
    rows, width = query.shape
    nz, plane = lax.axis_size("mem") // 2, lax.axis_size("seq")
    gr = rows // block_ids.shape[0]
    blocks = 2 * nz
    dma = pltpu.SemaphoreType.DMA
    any_ = pl.BlockSpec(memory_space=pl.ANY)
    vmem = pl.BlockSpec(memory_space=pltpu.VMEM)
    smem = pl.BlockSpec(memory_space=pltpu.SMEM)
    heads = width // HD
    scratch = (
        [pltpu.VMEM((nz, 2, 2, rows, HD), BF16)]
        + [pltpu.VMEM((plane * rows, HD), BF16)] * 3
        + [pltpu.VMEM((plane, blocks, 2 * gr, 2 * HD), BF16)]
        + [pltpu.VMEM((blocks * 2 * plane, gr, HD), F32)] * 5
        + [pltpu.VMEM((rows, width), BF16)] * 4
        + [pltpu.VMEM((rows, width), F32)] * 2
        + [pltpu.VMEM((8, width), F32)]
        + [pltpu.VMEM((plane * rows, HD), BF16)] * 2
        + [pltpu.VMEM((8, width), F32)]
        + [pltpu.VMEM((plane, 8, rows), jnp.int32), pltpu.SMEM((plane, 8, rows), jnp.int32)]
        + [pltpu.VMEM((size, 8, HD), F32) for size in (plane, 2, nz)]
        + [dma((11,))]
        + [dma((plane,))] * 10
        + [dma((nz,))] * 4
        + [dma((size,)) for size in (plane, plane, 2, 2, nz, nz)]
    )
    mem_out, mem_dq, local_out, local_dq, gate = pl.pallas_call(
        functools.partial(kernel, nz, total_tokens),
        out_shape=(
            jax.ShapeDtypeStruct((rows, width), BF16),
            jax.ShapeDtypeStruct((rows, width), BF16),
            jax.ShapeDtypeStruct((rows, width), F32),
            jax.ShapeDtypeStruct((rows, width), F32),
            jax.ShapeDtypeStruct((8, HD), F32),
        ),
        in_specs=[any_] * 6 + [smem, smem],
        out_specs=(any_, any_, any_, any_, vmem),
        scratch_shapes=scratch,
        compiler_params=pltpu.CompilerParams(
            collective_id=0, has_side_effects=True, vmem_limit_bytes=56 * 1024 * 1024
        ),
    )(query, key, value, mem_key, mem_value, d_out, block_ids.T, gate_logit)
    out = (mem_out.astype(F32) + local_out).astype(BF16)
    d_query = (mem_dq.astype(F32) + local_dq).astype(BF16)
    return out, d_query, gate[0, :heads]


def solution(mesh):
    tokens = P(("seq", "mem"), None)

    def run(query, *rest):
        return jax.shard_map(
            functools.partial(body, query.shape[0]),
            mesh=mesh,
            in_specs=(tokens, tokens, tokens, P("mem", None), P("mem", None), tokens, P(), tokens),
            out_specs=(tokens, tokens, P()),
            check_vma=False,
        )(query, *rest)

    return run
```

time: 94.2 us -> 73.7 us (0.78)
  Pallas kernels: 87.5 us -> 68.6 us
  local copies, waits for them, and re-layouts: 5.27 us -> 1.19 us
  other arithmetic: 0 us -> 3.09 us
    pallas_call x1, Pallas kernels: 87.5 us -> 68.6 us  [body(): pl.pallas_call(functools.partial(kernel, nz, total_tokens), out_shape=(ja...]
    unnamed x5 -> x0, local copies, waits for them, and re-layouts: 4.09 us -> none
    convert_element_type x0 -> x1, other arithmetic: none -> 3.09 us  [body(): d_query = (mem_dq.astype(F32) + local_dq).astype(BF16)]
where the time goes in v3:
time: 73.7 us; the launch traced here: 73.5 us
  Pallas kernels  68.6 us (93%)
  other arithmetic  3.09 us (4%)
  local copies, waits for them, and re-layouts  1.19 us (2%)
    pallas_call x1, Pallas kernels, body(): pl.pallas_call(functools.partial(kernel, nz, total_tokens), out_shape=(ja...  68.6 us
    convert_element_type x1, other arithmetic, body(): d_query = (mem_dq.astype(F32) + local_dq).astype(BF16)  3.09 us

profile of v3, /device:TPU:1, one launch (start us, length us, event | category | flops | bytes accessed | tf_op | source)
XLA Modules:
  0.0 73.5 jit_solution(5259071836620612145)
XLA Ops:
  0.6 68.6 %shard_map.103 = (bf16[128,2048]{1,0:T(8,128)(2,1)}, bf16[128,2048]{1,0:T(8,128)(2,1)}, f32[128,2048]{1,0:T(8,128)}, f32[128,2048]{1,0:T(8,128)}, f32[8,128]{1,0:T(8,128)}) custom-call(bf16[128,2048]{1,0:T(8,128)(2,1)} %q_hbm.1, bf16[128,2048]{1,0:T(8,128)(2,1)} %k_hbm.1, bf16[128,2048]{1,0:T(8,128)(2,1)} %v_hbm.1, bf16[128,2048]{1,0:T(8,128)(2,1)} %mk_hbm.1, ...), custom_call_target="tpu_custom_call" | custom-call | tf_op jit(solution)/shard_map/pallas_call | solution.py:491
  69.2 3.1 %add_convert_fusion = (bf16[128,2048]{1,0:T(8,128)(2,1)}, bf16[128,2048]{1,0:T(8,128)(2,1)}) fusion(f32[128,2048]{1,0:T(8,128)} %get-tuple-element.11, bf16[128,2048]{1,0:T(8,128)(2,1)} %get-tuple-element.10, f32[128,2048]{1,0:T(8,128)} %get-tuple-element.9, bf16[128,2048]{1,0:T(8,128)(2,1)} %get-tuple-element.8), kind=kLoop, calls=%fused_computation | loop fusion | flops 1572864 | bytes 4194304 | tf_op jit(solution)/shard_map/convert_element_type | solution.py:508
  72.3 1.2 %slice_bitcast_fusion = f32[16]{0:T(128)} fusion(f32[8,128]{1,0:T(8,128)} %get-tuple-element.12), kind=kLoop, calls=%fused_computation.2 | loop fusion | bytes 128 | tf_op jit(solution)/shard_map/squeeze | solution.py:509

commit v4 on v3

v4 whole, which is shorter than its diff:
```python
import functools
import math

import jax
import jax.numpy as jnp
from jax import lax
from jax.experimental import pallas as pl
from jax.experimental.pallas import tpu as pltpu
from jax.sharding import PartitionSpec as P

HD = 128
MESH = pl.DeviceIdType.MESH
F32 = jnp.float32
BF16 = jnp.bfloat16


def dot_nt(a, b):
    return lax.dot_general(a, b, (((1,), (1,)), ((), ())), preferred_element_type=F32)


def dot_nn(a, b):
    return jnp.dot(a, b, preferred_element_type=F32)


def row_sum(a):
    return jnp.sum(a, axis=-1, keepdims=True)


def kernel(
    nz, total_tokens,
    q_hbm, k_hbm, v_hbm, mk_hbm, mv_hbm, d_hbm, ids_ref, gl_ref,
    rm, rq, lo_hbm, ldq_hbm, gg_ref,
    kv, qs, gs, md, qg, mg, hots, pf, sh0, sh1, dt, po, da, db, ls, dl,
    qh, kh, vh, dh, lo, ldq, lacc, so, sd, gx, codes, codes_sm, rr, ry, rz,
    loc,
    q_s, q_r, d_s, d_r, c_s, c_r, m_s, m_r, g_s, g_r,
    z_s, z_r, b_s, b_r,
    rr_s, rr_r, ry_s, ry_r, rz_s, rz_r,
):
    rows, width = q_hbm.shape
    heads = width // HD
    plane = qg.shape[0]
    groups = ids_ref.shape[1]
    gr = rows // groups
    scale = HD ** -0.5

    s = lax.axis_index("seq")
    m = lax.axis_index("mem")
    z, c = m // 2, lax.rem(m, 2)
    toward = 1 - 2 * c

    def at_plane(step):
        return (lax.rem(s + step, plane), m)

    def at_z(step):
        return (s, lax.rem(z + step + nz, nz) * 2 + c)

    def at_sib(step):
        return (s, z * 2 + 1 - c)

    sib = at_sib(1)

    def cols_of(p):
        return pl.ds(pl.multiple_of(p * HD, HD), HD)

    def rows_of(p):
        return pl.ds(pl.multiple_of(p * rows, rows), rows)

    own = [
        pltpu.make_async_copy(src, dst, loc.at[i])
        for i, (src, dst) in enumerate((
            (mk_hbm.at[:, cols_of(s)], kv.at[z, c, 0]),
            (mv_hbm.at[:, cols_of(s)], kv.at[z, c, 1]),
            (q_hbm, qh),
            (d_hbm, dh),
            (k_hbm, kh),
            (v_hbm, vh),
        ))
    ]
    for cp in own:
        cp.start()

    barrier = pltpu.get_barrier_semaphore()

    def greet(dev):
        pl.semaphore_signal(barrier, inc=1, device_id=dev, device_id_type=MESH)

    greet(sib)
    for step in (1, -1, 2, -2):
        greet(at_z(step))

    def greet_plane(step, carry):
        greet(at_plane(step))
        return carry

    lax.fori_loop(1, plane, greet_plane, 0)

    pl.semaphore_wait(barrier, plane - 1 + 5)

    def plane_copy(src, dst, send, recv, step):
        return pltpu.make_async_remote_copy(
            src_ref=src, dst_ref=dst, send_sem=send.at[step], recv_sem=recv.at[step],
            device_id=at_plane(step), device_id_type=MESH,
        )

    def queries(step, p, q):
        return (
            plane_copy(codes.at[q], codes.at[q], c_s, c_r, step),
            plane_copy(qh.at[:, cols_of(p)], qs.at[rows_of(q)], q_s, q_r, step),
        )

    def grads(step, p, q):
        return (plane_copy(dh.at[:, cols_of(p)], gs.at[rows_of(q)], d_s, d_r, step),)

    def each_peer(make, sending, act):
        def go(step, carry):
            if sending:
                copies = make(step, lax.rem(s + step, plane), s)
            else:
                copies = make(step, s, lax.rem(s + plane - step, plane))
            for cp in copies:
                act(cp)
            return carry

        lax.fori_loop(1, plane, go, 0)

    last = nz - 1

    def origin(n):
        away = (n + 1) // 2 * toward
        return lax.rem(z + nz + jnp.where(lax.rem(n, 2) == 1, -away, away), nz)

    def along_z(o, n, step, part):
        return pltpu.make_async_remote_copy(
            src_ref=kv.at[o, c, part], dst_ref=kv.at[o, c, part],
            send_sem=z_s.at[part * nz + n], recv_sem=z_r.at[part * nz + n],
            device_id=at_z(step), device_id_type=MESH,
        )

    def across(o, who):
        return pltpu.make_async_remote_copy(
            src_ref=kv.at[o, who], dst_ref=kv.at[o, who], send_sem=b_s.at[o], recv_sem=b_r.at[o],
            device_id=sib, device_id_type=MESH,
        )

    def spread_z(o, hops, part):
        @pl.when(2 * hops + 3 <= last)
        def _():
            along_z(o[0], 2 * hops + 3, 2 * toward, part).start()

        @pl.when(2 * hops + 4 <= last)
        def _():
            along_z(o[1], 2 * hops + 4, -2 * toward, part).start()

        along_z(o[0], 2 * hops + 1, toward, part).start()
        along_z(o[1], 2 * hops + 2, -toward, part).start()

    def arrive(n):
        o = origin(n)
        along_z(o, n, 1, 0).wait_recv()
        along_z(o, n, 1, 1).wait_recv()
        across(o, c).start()

    def drain(n, carry):
        along_z(z, n, 1, 0).wait_send()
        along_z(z, n, 1, 1).wait_send()
        across(origin(n), c).wait_send()
        return carry

    my_gate = gx.at[:, cols_of(s)]
    slots_b = 2 * plane
    srows = slots_b * gr

    cube = (slots_b, gr, HD)
    def blocks_of(planes):
        return [(o, blk) for o in planes for blk in range(2)]

    def forward(planes):
        todo = blocks_of(planes)
        sc = [dot_nt(qg[:, o * 2 + blk].reshape(srows, HD), kv[o, blk, 0]) * scale for o, blk in todo]
        peak = [jnp.max(a, axis=-1, keepdims=True) for a in sc]
        e = [jnp.exp(a - b) for a, b in zip(sc, peak)]
        tot = [row_sum(a) for a in e]
        p = [a * (1.0 / b) for a, b in zip(e, tot)]
        for i, (o, blk) in enumerate(todo):
            sl = pl.ds((o * 2 + blk) * slots_b, slots_b)
            pf[o * 2 + blk] = p[i]
            ls[sl] = jnp.broadcast_to(peak[i] + jnp.log(tot[i]), (srows, HD)).reshape(cube)
            po[sl] = dot_nn(p[i].astype(BF16), kv[o, blk, 1]).reshape(cube)

    def backward(planes):
        todo = blocks_of(planes)
        dp = [dot_nt(mg[:, o * 2 + blk].reshape(srows, HD), kv[o, blk, 1]) for o, blk in todo]
        p = [pf[o * 2 + blk] for o, blk in todo]
        delta = [row_sum(a * b) for a, b in zip(p, dp)]
        dsb = [(a * (b - d)).astype(BF16) for a, b, d in zip(p, dp, delta)]
        for i, (o, blk) in enumerate(todo):
            sl = pl.ds((o * 2 + blk) * slots_b, slots_b)
            dl[sl] = jnp.broadcast_to(delta[i], (srows, HD)).reshape(cube)
            db[sl] = dot_nn(p[i].astype(BF16), kv[o, blk, 0]).reshape(cube)
            da[sl] = dot_nn(dsb[i], kv[o, blk, 0]).reshape(cube)

    per_pick = 4

    def pick_q(i, carry):
        lane = lax.broadcasted_iota(jnp.int32, (1, rows), 1) & (gr - 1)
        count = qg.shape[1] * 2 * gr
        at = lax.broadcasted_iota(jnp.int32, (count, rows), 0)
        hot = []
        for j in range(per_pick):
            d = i * per_pick + j
            c0, c1 = codes[d, 0:1, :], codes[d, 1:2, :]
            t0 = ((c0 // (2 * plane)) * 2 + (c0 & 1)) * gr + lane
            t1 = ((c1 // (2 * plane)) * 2 + (c1 & 1)) * gr + lane
            hot.append(jnp.where((at == t0) | (at == t1), 1.0, 0.0).astype(BF16))
        for j in range(per_pick):
            d = i * per_pick + j
            hots[d] = hot[j]
            qg[d] = dot_nn(hot[j], qs[rows_of(d), :]).astype(BF16).reshape(qg.shape[1], 2 * gr, HD)
        return carry

    def pick_d(i, carry):
        for j in range(per_pick):
            d = i * per_pick + j
            here_ = rows_of(d)
            gated = (my_gate[0:1, :] * gs[here_, :].astype(F32)).astype(BF16)
            md[here_, :] = gated
            mg[d] = dot_nn(hots[d], gated).astype(BF16).reshape(mg.shape[1], 2 * gr, HD)
        return carry

    ahead = 4

    def local(i):
        ri = lax.broadcasted_iota(jnp.int32, (rows, rows), 0)
        ci = lax.broadcasted_iota(jnp.int32, (rows, rows), 1)
        cols = [pl.ds(pl.multiple_of(i * (ahead * HD) + h * HD, HD), HD) for h in range(ahead)]
        kk = [kh[:, a] for a in cols]
        vv = [vh[:, a] for a in cols]
        g = [dh[:, a].astype(F32) for a in cols]
        ld = [((1.0 - gx[0:1, a]) * b).astype(BF16) for a, b in zip(cols, g)]
        sc = [jnp.where(ri >= ci, dot_nt(qh[:, a], b) * scale, -1e30) for a, b in zip(cols, kk)]
        dp = [dot_nt(a, b) for a, b in zip(ld, vv)]
        e = [jnp.exp(a - jnp.max(a, axis=-1, keepdims=True)) for a in sc]
        p = [a * (1.0 / row_sum(a)) for a in e]
        o = [dot_nn(a.astype(BF16), b) for a, b in zip(p, vv)]
        delta = [row_sum(a.astype(F32) * b) for a, b in zip(ld, o)]
        ds = [(a * (b - d)).astype(BF16) for a, b, d in zip(p, dp, delta)]
        for h, a in enumerate(cols):
            lo[:, a] = (1.0 - gx[0:1, a]) * o[h]
            ldq[:, a] = dot_nn(ds[h], kk[h]) * scale
            lacc[:, a] = jnp.sum((g[h] * o[h]).reshape(rows // 8, 8, HD), axis=0)

    home = [
        pltpu.make_async_copy(lo, lo_hbm, loc.at[0]),
        pltpu.make_async_copy(ldq, ldq_hbm, loc.at[1]),
    ]

    for part in range(2):
        own[part].wait()
        spread_z((z, z), 0, part)
    across(z, c).start()
    g_row = lax.broadcasted_iota(jnp.int32, (groups, rows), 0)
    g_tok = lax.broadcasted_iota(jnp.int32, (groups, rows), 1) // gr
    zero = jnp.zeros((groups, rows), jnp.int32)
    a0, a1, i0, i1 = zero, zero, zero, zero
    for g in range(groups):
        b0, b1 = ids_ref[0, g], ids_ref[1, g]
        a0, a1 = jnp.where(g_row == g, b0, a0), jnp.where(g_row == g, b1, a1)
        i0, i1 = jnp.where(g_tok == g, b0, i0), jnp.where(g_tok == g, b1, i1)
    one = zero + 1
    earlier = g_row < g_tok
    r0 = jnp.sum(jnp.where(earlier & ((a0 == i0) | (a1 == i0)), one, zero), axis=0, keepdims=True)
    r1 = jnp.sum(jnp.where(earlier & ((a0 == i1) | (a1 == i1)), one, zero), axis=0, keepdims=True)
    code0 = i0[0:1] * (2 * plane) + s * 2 + r0
    code1 = i1[0:1] * (2 * plane) + s * 2 + r1
    first = lax.broadcasted_iota(jnp.int32, (8, rows), 0) == 0
    codes[s] = jnp.where(first, jnp.broadcast_to(code0, (8, rows)), jnp.broadcast_to(code1, (8, rows)))

    for j in range(heads):
        logit = jnp.full((8, HD), gl_ref[j], F32)
        gx[:, j * HD:(j + 1) * HD] = 1.0 / (1.0 + jnp.exp(-logit))

    own[2].wait()
    own[3].wait()

    each_peer(queries, True, lambda cp: cp.start())
    each_peer(grads, True, lambda cp: cp.start())
    keep = [
        pltpu.make_async_copy(qh.at[:, cols_of(s)], qs.at[rows_of(s)], loc.at[6]),
        pltpu.make_async_copy(dh.at[:, cols_of(s)], gs.at[rows_of(s)], loc.at[7]),
    ]
    for cp in keep:
        cp.start()
    own[4].wait()
    own[5].wait()

    turns = nz // 4
    ready, ready_d = 2, 3

    def back_pair(i, carry):
        backward([origin(2 * i), origin(2 * i + 1)])
        return carry

    def turn(t, carry):
        far = 4 * t - 1

        @pl.when(t < turns)
        def _():
            a, b = origin(far), origin(far + 1)
            for part in range(2):
                along_z(a, far, 1, part).wait_recv()
                along_z(b, far + 1, 1, part).wait_recv()
                spread_z((a, b), 2 * t, part)
            across(a, c).start()
            across(b, c).start()

        @pl.when(t <= turns)
        def _():
            arrive(far - 2)
            arrive(far - 1)

        @pl.when(t == turns)
        def _():
            arrive(far)

        @pl.when(t <= 2)
        def _():
            for i in range(heads // ahead // 2):
                local((t - 1) * (heads // ahead // 2) + i)

        @pl.when(t == 2)
        def _():
            for cp in home:
                cp.start()

        @pl.when(t == ready)
        def _():
            each_peer(queries, False, lambda cp: cp.wait_recv())
            keep[0].wait()
            to_smem = pltpu.make_async_copy(codes, codes_sm, loc.at[8])
            to_smem.start()
            lax.fori_loop(0, plane // per_pick, pick_q, 0)
            to_smem.wait()

        @pl.when(t == ready_d)
        def _():
            each_peer(grads, False, lambda cp: cp.wait_recv())
            keep[1].wait()
            lax.fori_loop(0, plane // per_pick, pick_d, 0)

        def reached(t):
            return jnp.maximum(jnp.minimum(jnp.minimum(2 * t - 1, nz // 2), 4 * (t - ready + 1)), 0)

        def step(i, carry):
            across(origin(2 * i), 1 - c).wait_recv()
            across(origin(2 * i + 1), 1 - c).wait_recv()
            forward([origin(2 * i), origin(2 * i + 1)])
            return carry

        lax.fori_loop(reached(t - 1), reached(t), step, 0)

        @pl.when(t <= turns)
        def _():
            lax.fori_loop(1 * jnp.maximum(t - ready_d, 0), 1 * jnp.maximum(t - ready_d + 1, 0), back_pair, 0)

        return carry

    lax.fori_loop(1, turns + 2, turn, 0)
    early = 1 * (turns - ready_d + 1)

    groups_ = range(groups)

    def slots_of(base):
        return (
            [codes_sm[base, 0, g * gr] for g in groups_],
            [codes_sm[base, 1, g * gr] for g in groups_],
        )

    def cut(a):
        return [a[i * gr:(i + 1) * gr] for i in groups_]

    def mix_out(base):
        at = rows_of(base)
        d0, d1 = slots_of(base)
        l0, l1 = [ls[d] for d in d0], [ls[d] for d in d1]
        peak = [jnp.maximum(a, b) for a, b in zip(l0, l1)]
        e0 = [jnp.exp(a - b) for a, b in zip(l0, peak)]
        e1 = [jnp.exp(a - b) for a, b in zip(l1, peak)]
        inv = [1.0 / (a + b) for a, b in zip(e0, e1)]
        s0 = [a * b for a, b in zip(e0, inv)]
        s1 = [a * b for a, b in zip(e1, inv)]
        mo = [a * po[i] + b * po[j] for a, b, i, j in zip(s0, s1, d0, d1)]
        prod = [a * b for a, b in zip(cut(md[at, :].astype(F32)), mo)]
        so[at, :] = (my_gate[0:1, :] * jnp.concatenate(mo, axis=0)).astype(BF16)
        sh0[at, :] = jnp.concatenate(s0, axis=0)
        sh1[at, :] = jnp.concatenate(s1, axis=0)
        dt[at, :] = jnp.concatenate([jnp.broadcast_to(row_sum(a), (gr, HD)) for a in prod], axis=0)
        return sum([a * b for a, b in zip(cut(gs[at, :].astype(F32)), mo)])

    def mix_dq(base):
        at = rows_of(base)
        d0, d1 = slots_of(base)
        delta = cut(dt[at, :])
        dq = [a * (da[i] + (dl[i] - d) * db[i]) for a, i, d in zip(cut(sh0[at, :]), d0, delta)]
        dq = [q + a * (da[i] + (dl[i] - d) * db[i]) for q, a, i, d in zip(dq, cut(sh1[at, :]), d1, delta)]
        sd[at, :] = (scale * jnp.concatenate(dq, axis=0)).astype(BF16)

    def out_back(p, q, step):
        return plane_copy(so.at[rows_of(p)], rm.at[:, cols_of(q)], m_s, m_r, step)

    def dq_back(p, q, step):
        return plane_copy(sd.at[rows_of(p)], rq.at[:, cols_of(q)], g_s, g_r, step)

    own_back = [
        pltpu.make_async_copy(so.at[rows_of(s)], rm.at[:, cols_of(s)], loc.at[9]),
        pltpu.make_async_copy(sd.at[rows_of(s)], rq.at[:, cols_of(s)], loc.at[10]),
    ]

    per_merge = 2

    def merge_out(i, acc):
        for j in range(per_merge):
            base = lax.rem(s + i * per_merge + j + plane // 2, plane)
            acc = acc + mix_out(base)
        for j in range(per_merge):
            step = lax.rem(i * per_merge + j + plane // 2, plane)
            base = lax.rem(s + step, plane)

            @pl.when(step > 0)
            def _(base=base, step=step):
                out_back(base, s, step).start()

        return acc

    acc = lax.fori_loop(0, plane // per_merge, merge_out, jnp.zeros((gr, HD), F32))
    own_back[0].start()

    lane = lax.broadcasted_iota(jnp.int32, (8, HD), 1)
    term = jnp.zeros((8, HD), F32)
    gates = jnp.zeros((8, HD), F32)

    def spread(a):
        return jnp.broadcast_to(jnp.sum(row_sum(a), axis=0, keepdims=True), (8, HD))

    for j in range(heads):
        cols = slice(j * HD, (j + 1) * HD)
        term = jnp.where(lane == j, -spread(lacc[:, cols]), term)
        gates = jnp.where(lane == j, gx[:, cols], gates)
    term = term + jnp.where(lane == s, spread(acc), 0.0)
    term = term * gates * (1.0 - gates) * (1.0 / math.sqrt(total_tokens))

    def peers(buf, place, at, send, recv):
        size = buf.shape[0]

        def make(step, src):
            return pltpu.make_async_remote_copy(
                src_ref=buf.at[src], dst_ref=buf.at[src], send_sem=send.at[step], recv_sem=recv.at[step],
                device_id=at(step), device_id_type=MESH,
            )

        def start(step, carry):
            make(step, place).start()
            return carry

        def wait(step, carry):
            make(step, lax.rem(place + size - step, size)).wait_recv()
            make(step, place).wait_send()
            return carry

        def post(a):
            buf[place] = a
            lax.fori_loop(1, size, start, 0)

        def total():
            lax.fori_loop(1, size, wait, 0)
            out = buf[0]
            for i in range(1, size):
                out = out + buf[i]
            return out

        return post, total

    post_z, total_z = peers(rz, z, at_z, rz_s, rz_r)
    post_c, total_c = peers(ry, c, at_sib, ry_s, ry_r)
    post_p, total_p = peers(rr, s, at_plane, rr_s, rr_r)
    post_z(term)

    lax.fori_loop(early, nz // 2, back_pair, 0)
    def merge_dq(i, carry):
        for j in range(per_merge):
            mix_dq(lax.rem(s + i * per_merge + j + plane // 2, plane))
        for j in range(per_merge):
            step = lax.rem(i * per_merge + j + plane // 2, plane)
            base = lax.rem(s + step, plane)

            @pl.when(step > 0)
            def _(base=base, step=step):
                dq_back(base, s, step).start()

        return carry

    lax.fori_loop(0, plane // per_merge, merge_dq, 0)
    own_back[1].start()

    post_c(total_z())
    post_p(total_c())

    each_peer(queries, True, lambda cp: cp.wait_send())
    each_peer(grads, True, lambda cp: cp.wait_send())
    across(z, c).wait_send()
    lax.fori_loop(1, nz, drain, 0)
    for cp in home:
        cp.wait()

    def taken(step, carry):
        p = lax.rem(s + plane - step, plane)
        out_back(s, s, step).wait_send()
        dq_back(s, s, step).wait_send()
        out_back(s, p, step).wait_recv()
        dq_back(s, p, step).wait_recv()
        return carry

    lax.fori_loop(1, plane, taken, 0)
    for cp in own_back:
        cp.wait()
    gg_ref[...] = total_p()


def body(total_tokens, query, key, value, mem_key, mem_value, block_ids, gate_logit, d_out):
    rows, width = query.shape
    nz, plane = lax.axis_size("mem") // 2, lax.axis_size("seq")
    gr = rows // block_ids.shape[0]
    blocks = 2 * nz
    dma = pltpu.SemaphoreType.DMA
    any_ = pl.BlockSpec(memory_space=pl.ANY)
    vmem = pl.BlockSpec(memory_space=pltpu.VMEM)
    smem = pl.BlockSpec(memory_space=pltpu.SMEM)
    heads = width // HD
    scratch = (
        [pltpu.VMEM((nz, 2, 2, rows, HD), BF16)]
        + [pltpu.VMEM((plane * rows, HD), BF16)] * 3
        + [pltpu.VMEM((plane, blocks, 2 * gr, HD), BF16)] * 2
        + [pltpu.VMEM((plane, blocks * 2 * gr, rows), BF16)]
        + [pltpu.VMEM((blocks, plane * 2 * gr, HD), F32)]
        + [pltpu.VMEM((plane * rows, HD), F32)] * 3
        + [pltpu.VMEM((blocks * 2 * plane, gr, HD), F32)] * 5
        + [pltpu.VMEM((rows, width), BF16)] * 4
        + [pltpu.VMEM((rows, width), F32)] * 2
        + [pltpu.VMEM((8, width), F32)]
        + [pltpu.VMEM((plane * rows, HD), BF16)] * 2
        + [pltpu.VMEM((8, width), F32)]
        + [pltpu.VMEM((plane, 8, rows), jnp.int32), pltpu.SMEM((plane, 8, rows), jnp.int32)]
        + [pltpu.VMEM((size, 8, HD), F32) for size in (plane, 2, nz)]
        + [dma((11,))]
        + [dma((plane,))] * 10
        + [dma((2 * nz,))] * 2
        + [dma((nz,))] * 2
        + [dma((size,)) for size in (plane, plane, 2, 2, nz, nz)]
    )
    mem_out, mem_dq, local_out, local_dq, gate = pl.pallas_call(
        functools.partial(kernel, nz, total_tokens),
        out_shape=(
            jax.ShapeDtypeStruct((rows, width), BF16),
            jax.ShapeDtypeStruct((rows, width), BF16),
            jax.ShapeDtypeStruct((rows, width), F32),
            jax.ShapeDtypeStruct((rows, width), F32),
            jax.ShapeDtypeStruct((8, HD), F32),
        ),
        in_specs=[any_] * 6 + [smem, smem],
        out_specs=(any_, any_, any_, any_, vmem),
        scratch_shapes=scratch,
        compiler_params=pltpu.CompilerParams(
            collective_id=0, has_side_effects=True, vmem_limit_bytes=56 * 1024 * 1024
        ),
    )(query, key, value, mem_key, mem_value, d_out, block_ids.T, gate_logit)
    out = (mem_out.astype(F32) + local_out).astype(BF16)
    d_query = (mem_dq.astype(F32) + local_dq).astype(BF16)
    return out, d_query, gate[0, :heads]


def solution(mesh):
    tokens = P(("seq", "mem"), None)

    def run(query, *rest):
        return jax.shard_map(
            functools.partial(body, query.shape[0]),
            mesh=mesh,
            in_specs=(tokens, tokens, tokens, P("mem", None), P("mem", None), tokens, P(), tokens),
            out_specs=(tokens, tokens, P()),
            check_vma=False,
        )(query, *rest)

    return run
```

time: 73.7 us -> 66.4 us (0.901)
  Pallas kernels: 68.6 us -> 61.3 us
    pallas_call x1, Pallas kernels: 68.6 us -> 61.3 us  [body(): pl.pallas_call(functools.partial(kernel, nz, total_tokens), out_shape=(ja...]
where the time goes in v4:
time: 66.4 us; the launch traced here: 66.2 us
  Pallas kernels  61.3 us (92%)
  other arithmetic  3.09 us (5%)
  local copies, waits for them, and re-layouts  1.19 us (2%)
    pallas_call x1, Pallas kernels, body(): pl.pallas_call(functools.partial(kernel, nz, total_tokens), out_shape=(ja...  61.3 us
    convert_element_type x1, other arithmetic, body(): d_query = (mem_dq.astype(F32) + local_dq).astype(BF16)  3.09 us

profile of v4, /device:TPU:1, one launch (start us, length us, event | category | flops | bytes accessed | tf_op | source)
XLA Modules:
  0.0 66.2 jit_solution(12021069636012263841)
XLA Ops:
  0.6 61.3 %shard_map.103 = (bf16[128,2048]{1,0:T(8,128)(2,1)}, bf16[128,2048]{1,0:T(8,128)(2,1)}, f32[128,2048]{1,0:T(8,128)}, f32[128,2048]{1,0:T(8,128)}, f32[8,128]{1,0:T(8,128)}) custom-call(bf16[128,2048]{1,0:T(8,128)(2,1)} %q_hbm.1, bf16[128,2048]{1,0:T(8,128)(2,1)} %k_hbm.1, bf16[128,2048]{1,0:T(8,128)(2,1)} %v_hbm.1, bf16[128,2048]{1,0:T(8,128)(2,1)} %mk_hbm.1, ...), custom_call_target="tpu_custom_call" | custom-call | tf_op jit(solution)/shard_map/pallas_call | solution.py:560
  61.9 3.1 %add_convert_fusion = (bf16[128,2048]{1,0:T(8,128)(2,1)}, bf16[128,2048]{1,0:T(8,128)(2,1)}) fusion(f32[128,2048]{1,0:T(8,128)} %get-tuple-element.11, bf16[128,2048]{1,0:T(8,128)(2,1)} %get-tuple-element.10, f32[128,2048]{1,0:T(8,128)} %get-tuple-element.9, bf16[128,2048]{1,0:T(8,128)(2,1)} %get-tuple-element.8), kind=kLoop, calls=%fused_computation | loop fusion | flops 1572864 | bytes 4194304 | tf_op jit(solution)/shard_map/convert_element_type | solution.py:577
  65.0 1.2 %slice_bitcast_fusion = f32[16]{0:T(128)} fusion(f32[8,128]{1,0:T(8,128)} %get-tuple-element.12), kind=kLoop, calls=%fused_computation.2 | loop fusion | bytes 128 | tf_op jit(solution)/shard_map/squeeze | solution.py:578

commit v5 on v4

--- a/solution.py
+++ b/solution.py
@@ -143,7 +143,7 @@
             device_id=sib, device_id_type=MESH,
         )
 
-    def spread_z(o, hops, part):
+    def two_on(o, hops, part):
         @pl.when(2 * hops + 3 <= last)
         def _():
             along_z(o[0], 2 * hops + 3, 2 * toward, part).start()
@@ -152,8 +152,10 @@
         def _():
             along_z(o[1], 2 * hops + 4, -2 * toward, part).start()
 
-        along_z(o[0], 2 * hops + 1, toward, part).start()
-        along_z(o[1], 2 * hops + 2, -toward, part).start()
+    def one_on(o, hops):
+        for part in range(2):
+            along_z(o[0], 2 * hops + 1, toward, part).start()
+            along_z(o[1], 2 * hops + 2, -toward, part).start()
 
     def arrive(n):
         o = origin(n)
@@ -246,8 +248,8 @@
         delta = [row_sum(a.astype(F32) * b) for a, b in zip(ld, o)]
         ds = [(a * (b - d)).astype(BF16) for a, b, d in zip(p, dp, delta)]
         for h, a in enumerate(cols):
-            lo[:, a] = (1.0 - gx[0:1, a]) * o[h]
-            ldq[:, a] = dot_nn(ds[h], kk[h]) * scale
+            lo[:, a] = ((1.0 - gx[0:1, a]) * o[h]).astype(BF16)
+            ldq[:, a] = (dot_nn(ds[h], kk[h]) * scale).astype(BF16)
             lacc[:, a] = jnp.sum((g[h] * o[h]).reshape(rows // 8, 8, HD), axis=0)
 
     home = [
@@ -257,7 +259,8 @@
 
     for part in range(2):
         own[part].wait()
-        spread_z((z, z), 0, part)
+        two_on((z, z), 0, part)
+    one_on((z, z), 0)
     across(z, c).start()
     g_row = lax.broadcasted_iota(jnp.int32, (groups, rows), 0)
     g_tok = lax.broadcasted_iota(jnp.int32, (groups, rows), 1) // gr
@@ -295,7 +298,7 @@
     own[5].wait()
 
     turns = nz // 4
-    ready, ready_d = 2, 3
+    ready, ready_d = 2, 4
 
     def back_pair(i, carry):
         backward([origin(2 * i), origin(2 * i + 1)])
@@ -310,7 +313,8 @@
             for part in range(2):
                 along_z(a, far, 1, part).wait_recv()
                 along_z(b, far + 1, 1, part).wait_recv()
-                spread_z((a, b), 2 * t, part)
+                two_on((a, b), 2 * t, part)
+            one_on((a, b), 2 * t)
             across(a, c).start()
             across(b, c).start()
 
@@ -545,7 +549,7 @@
         + [pltpu.VMEM((plane * rows, HD), F32)] * 3
         + [pltpu.VMEM((blocks * 2 * plane, gr, HD), F32)] * 5
         + [pltpu.VMEM((rows, width), BF16)] * 4
-        + [pltpu.VMEM((rows, width), F32)] * 2
+        + [pltpu.VMEM((rows, width), BF16)] * 2
         + [pltpu.VMEM((8, width), F32)]
         + [pltpu.VMEM((plane * rows, HD), BF16)] * 2
         + [pltpu.VMEM((8, width), F32)]
@@ -562,8 +566,8 @@
         out_shape=(
             jax.ShapeDtypeStruct((rows, width), BF16),
             jax.ShapeDtypeStruct((rows, width), BF16),
-            jax.ShapeDtypeStruct((rows, width), F32),
-            jax.ShapeDtypeStruct((rows, width), F32),
+            jax.ShapeDtypeStruct((rows, width), BF16),
+            jax.ShapeDtypeStruct((rows, width), BF16),
             jax.ShapeDtypeStruct((8, HD), F32),
         ),
         in_specs=[any_] * 6 + [smem, smem],
@@ -573,8 +577,8 @@
             collective_id=0, has_side_effects=True, vmem_limit_bytes=56 * 1024 * 1024
         ),
     )(query, key, value, mem_key, mem_value, d_out, block_ids.T, gate_logit)
-    out = (mem_out.astype(F32) + local_out).astype(BF16)
-    d_query = (mem_dq.astype(F32) + local_dq).astype(BF16)
+    out = (mem_out.astype(F32) + local_out.astype(F32)).astype(BF16)
+    d_query = (mem_dq.astype(F32) + local_dq.astype(F32)).astype(BF16)
     return out, d_query, gate[0, :heads]
 
 

time: 66.4 us -> 65.6 us (0.988)
  no operation moved by 1% of the time
where the time goes in v5:
time: 65.6 us; the launch traced here: 65.4 us
  Pallas kernels  60.7 us (93%)
  other arithmetic  2.88 us (4%)
  local copies, waits for them, and re-layouts  1.19 us (2%)
    pallas_call x1, Pallas kernels, body(): pl.pallas_call(functools.partial(kernel, nz, total_tokens), out_shape=(ja...  60.7 us
    convert_element_type x1, other arithmetic, body(): d_query = (mem_dq.astype(F32) + local_dq.astype(F32)).astype(BF16)  2.88 us

profile of v5, /device:TPU:1, one launch (start us, length us, event | category | flops | bytes accessed | tf_op | source)
XLA Modules:
  0.0 65.4 jit_solution(2186785618903180363)
XLA Ops:
  0.6 60.7 %shard_map.103 = (bf16[128,2048]{1,0:T(8,128)(2,1)}, bf16[128,2048]{1,0:T(8,128)(2,1)}, bf16[128,2048]{1,0:T(8,128)(2,1)}, bf16[128,2048]{1,0:T(8,128)(2,1)}, f32[8,128]{1,0:T(8,128)}) custom-call(bf16[128,2048]{1,0:T(8,128)(2,1)} %q_hbm.1, bf16[128,2048]{1,0:T(8,128)(2,1)} %k_hbm.1, bf16[128,2048]{1,0:T(8,128)(2,1)} %v_hbm.1, bf16[128,2048]{1,0:T(8,128)(2,1)} %mk_hbm.1, ...), custom_call_target="tpu_custom_call" | custom-call | tf_op jit(solution)/shard_map/pallas_call | solution.py:564
  61.3 2.9 %add_convert_fusion = (bf16[128,2048]{1,0:T(8,128)(2,1)}, bf16[128,2048]{1,0:T(8,128)(2,1)}) fusion(bf16[128,2048]{1,0:T(8,128)(2,1)} %get-tuple-element.11, bf16[128,2048]{1,0:T(8,128)(2,1)} %get-tuple-element.10, bf16[128,2048]{1,0:T(8,128)(2,1)} %get-tuple-element.9, bf16[128,2048]{1,0:T(8,128)(2,1)} %get-tuple-element.8), kind=kLoop, calls=%fused_computation | loop fusion | flops 2097152 | bytes 3145728 | tf_op jit(solution)/shard_map/convert_element_type | solution.py:581
  64.2 1.2 %slice_bitcast_fusion = f32[16]{0:T(128)} fusion(f32[8,128]{1,0:T(8,128)} %get-tuple-element.12), kind=kLoop, calls=%fused_computation.2 | loop fusion | bytes 128 | tf_op jit(solution)/shard_map/squeeze | solution.py:582
